TPU v7x, 128 devices: a whole 4x4x4 slice. The times are simulated.
128 devices in a mesh: lon: 16 (over y, x_lo, core), lat: 8 (over x_hi, z).
Axes of the slice: x: 4 (x_hi: 2, x_lo: 2; x = x_hi * 2 + x_lo), y: 4, z: 4, core: 2. Of those that a mesh axis runs over, the one named last changes fastest.
Arguments:
- tracers: float32 [2, 48, 256, 4096], P(None, None, 'lat', 'lon'), may hold values from -6 to 6
- u_east: float32 [48, 256, 4096], P(None, 'lat', 'lon'), may hold values from -0.15 to 0.15
- v_north: float32 [48, 256, 4096], P(None, 'lat', 'lon'), may hold values from -0.15 to 0.15
- bottom: int32 [256, 4096], P('lat', 'lon'), may hold values from 0 to 48
Outputs:
- advanced: float32 [2, 48, 256, 4096], P(None, None, 'lat', 'lon')
All inputs are finite; a program needn't handle non-finite values.
Results may differ from a plain program's by a relative error of at most 0.0003.
Values sent between devices are 32-bit elements; how exact they have to be, the bound alone decides.
No kernel may reach another device: no remote copies, remote signals or barrier semaphores. Data moves between devices by JAX's collectives and lax.ppermute only.
A program may use at most 128 MiB of HBM per device.

v0:
```python
import functools

import jax
import jax.numpy as jnp
from jax import lax
from jax.experimental import pallas as pl
from jax.experimental.pallas import tpu as pltpu
from jax.sharding import PartitionSpec as P

LEV = 48
BANDS = LEV // 8
ROWS = 32
COLS = 256
GHOST = 3
PLANES = ROWS + 2 * GHOST
PAD = 8
DEEP = 64
DROW = 8
ITEMS = 11
DEPTHS = ITEMS * 2 * LEV
CORNERS = DEPTHS + 16
CORNER = LEV + 16
PACKED = CORNERS + CORNER
STRIP = 4 * 2 * LEV + ROWS
H_KAPPA = 0.06
V_KAPPA = 0.08
SHUT = 1e30
F32 = jnp.float32


def lanes():
    return lax.broadcasted_iota(jnp.int32, (8, 128), 1)


def turned(x, shift):
    return pltpu.roll(x, shift % 128 if isinstance(shift, int) else lax.rem(shift + 1024, 128), 1)


def gathered(x, index):
    return jnp.take_along_axis(x, index, axis=1)


def is_top():
    return lax.axis_index("lat") == lax.axis_size("lat") - 1


def is_even():
    return lax.axis_index("lat") % 2 == 0


def rows_kernel(x, up, vp, dp, first, second, sems):
    even = is_even()

    def fill(out, north, sem):
        def row(i):
            return jnp.where(north, ROWS - 1 - i, i) + GHOST

        def face(j):
            return jnp.where(north, ROWS - 1 - j, max(j - 1, 0)) + GHOST

        items = [(x.at[t], row(i), PAD) for t in range(2) for i in range(3)]
        items += [(vp, face(j), 0) for j in range(3)] + [(up, row(i), 0) for i in range(2)]
        for n, (ref, i, offset) in enumerate(items):
            for half in range(2):
                pltpu.make_async_copy(
                    ref.at[i, half, pl.ds(offset, LEV), :],
                    out.at[pl.ds((2 * n + half) * LEV, LEV), :],
                    sem,
                ).start()

    def finish(out, north, sem):
        all_items = out.at[pl.ds(0, DEPTHS), :]
        pltpu.make_async_copy(all_items, all_items, sem).wait()
        out[pl.ds(DEPTHS, 16), :] = jnp.zeros((16, 128), F32)
        for i in range(3):
            r = jnp.where(north, ROWS - 1 - i, i)
            for half in range(2):
                out[pl.ds(DEPTHS + 2 * i + half, 1), :] = dp[half, pl.ds(r + DROW, 1), :]

    odd = jnp.logical_not(even)
    fill(first, even, sems.at[0])
    fill(second, odd, sems.at[1])
    finish(first, even, sems.at[0])
    finish(second, odd, sems.at[1])

    @pl.when(is_top())
    def _():
        back = 127 - lanes()

        def turn(n, _):
            for k in range(BANDS):
                a = pl.ds(2 * n * LEV + 8 * k, 8)
                b = pl.ds((2 * n + 1) * LEV + 8 * k, 8)
                left, right = second[a, :], second[b, :]
                second[a, :] = gathered(right, back)
                second[b, :] = gathered(left, back)
            return 0

        lax.fori_loop(0, ITEMS, turn, 0)
        rows = gathered(second[pl.ds(DEPTHS, 8), :], back)
        for i in range(3):
            for half in range(2):
                source = 2 * i + 1 - half
                second[pl.ds(DEPTHS + 2 * i + half, 1), :] = rows[source : source + 1, :]


def load_kernel(tr, u, v, bottom, x, up, vp, dp, strip, sems):
    def start(r, _):
        for half in range(2):
            columns = pl.ds(128 * half, 128)
            pltpu.make_async_copy(
                tr.at[:, :, r, columns], x.at[:, r + GHOST, half, pl.ds(PAD, LEV), :], sems.at[0]
            ).start()
        return 0

    def start_flow(r, _, source=None, into=None, sem=None):
        for half in range(2):
            pltpu.make_async_copy(
                source.at[:, r, pl.ds(128 * half, 128)], into.at[r + GHOST, half], sem
            ).start()
        return 0

    lax.fori_loop(0, ROWS, functools.partial(start_flow, source=u, into=up, sem=sems.at[1]), 0)
    lax.fori_loop(0, ROWS, functools.partial(start_flow, source=v, into=vp, sem=sems.at[2]), 0)
    lax.fori_loop(0, ROWS, start, 0)

    depth = bottom[...].astype(F32)
    dp[...] = jnp.zeros_like(dp)
    for half in range(2):
        dp[half, pl.ds(DROW, ROWS), :] = depth[:, 128 * half : 128 * half + 128]
    strip_lane = lax.broadcasted_iota(jnp.int32, (ROWS, 128), 1)
    strip[pl.ds(8 * LEV, ROWS), :] = jnp.where(strip_lane < 64, depth[:, :128], depth[:, 128:])

    zeros = jnp.zeros((8, 128), F32)
    lane = lanes()

    def clear(i, _):
        for t in range(2):
            for half in range(2):
                x[t, i, half, pl.ds(0, 8), :] = zeros
                x[t, i, half, pl.ds(DEEP - 8, 8), :] = zeros
        return 0

    lax.fori_loop(0, PLANES, clear, 0)

    def pack(f, load):
        def one(k, _):
            for part in range(2):
                total = zeros
                for s in range(16):
                    a, b = load(part * 16 + s + GHOST, k)
                    both = turned(jnp.where(lane < 64, a, b), 8 * s + 3)
                    total = jnp.where(lane // 8 == s, both, total)
                strip[pl.ds((f * 2 + part) * LEV + 8 * k, 8), :] = total
            return 0

        lax.fori_loop(0, BANDS, one, 0)

    own = pl.ds(GHOST, ROWS)
    for n, ref in ((1, up), (2, vp)):
        pltpu.make_async_copy(ref.at[own], ref.at[own], sems.at[n]).wait()
        if n == 2:

            @pl.when(is_top())
            def _():
                for half in range(2):
                    vp[GHOST + ROWS - 1, half] = jnp.zeros((LEV, 128), F32)

        pack(n + 1, lambda i, k, ref=ref: [ref[i, half, pl.ds(8 * k, 8), :] for half in range(2)])
    whole = x.at[:, own, :, pl.ds(PAD, LEV), :]
    pltpu.make_async_copy(whole, whole, sems.at[0]).wait()
    for t in range(2):
        pack(t, lambda i, k, t=t: [x[t, i, half, pl.ds(PAD + 8 * k, 8), :] for half in range(2)])


def level_of(k):
    return (lax.broadcasted_iota(jnp.int32, (8, 128), 0) + 8 * k).astype(F32)


def above_of(k):
    level = level_of(k)
    return jnp.where(level > 0.0, level, 1e9) if k == 0 else level


def forth(speed, opened):
    return jnp.where(opened, jnp.maximum(speed, 0.0) + H_KAPPA, 0.0)


def back(speed, opened):
    return jnp.where(opened, H_KAPPA - jnp.minimum(speed, 0.0), 0.0)


def depth_row(dp, i, count):
    at = pl.ds(i - GHOST + DROW, 1)
    return [jnp.broadcast_to(dp[n, at, :], (8, 128)) for n in range(count)]


def make_faces(i, vp, dp, cr, ct):
    here, north = depth_row(dp, i, 2), depth_row(dp, i + 1, 2)
    for n in range(2):
        least = jnp.minimum(here[n], north[n])
        for k in range(BANDS):
            at = pl.ds(8 * k, 8)
            speed = vp[i, n, at, :]
            opened = level_of(k) < least
            cr[i, n, at, :] = forth(speed, opened)
            ct[i, n, at, :] = back(speed, opened)


def make_column(i, dp, ck):
    here = depth_row(dp, i, 2)
    for n in range(2):
        ck[i, n, pl.ds(0, 8), :] = jnp.zeros((8, 128), F32)
        for k in range(BANDS):
            ck[i, n, pl.ds(PAD + 8 * k, 8), :] = jnp.where(level_of(k) + 1.0 < here[n], V_KAPPA, 0.0)


def make_cells(rows, up, dp, edge_speed, cc, ce, cw, cr, ct, ck):
    lane = lanes()
    leasts = []
    for i, _, _ in rows:
        here = depth_row(dp, i, 3)
        east = [turned(h, -1) for h in here]
        leasts.append([jnp.minimum(here[n], jnp.where(lane == 127, east[n + 1], east[n])) for n in range(2)])
    for k in range(BANDS):
        at = pl.ds(8 * k, 8)
        for (i, part, slot), least in zip(rows, leasts):
            speeds = [jnp.where(level_of(k) < least[n], up[i, n, at, :], SHUT) for n in range(2)]
            a, b = [turned(speed, 1) for speed in speeds]
            outer = turned(edge_speed[part, at, :], -8 * slot - 2)
            wests = [jnp.where(lane == 0, outer, a), jnp.where(lane == 0, a, b)]
            for n in range(2):
                open_e, open_w = speeds[n] < SHUT, wests[n] < SHUT
                to_east = forth(speeds[n], open_e)
                from_east = back(speeds[n], open_e)
                ce[i, n, at, :] = from_east
                cw[i, n, at, :] = forth(wests[n], open_w)
                column = ck[i, n, pl.ds(PAD + 8 * k, 8), :] + ck[i, n, pl.ds(PAD + 8 * k - 1, 8), :]
                flows = (to_east + back(wests[n], open_w)) + (cr[i, n, at, :] + ct[i - 1, n, at, :])
                cc[i, n, at, :] = 1.0 - (flows + column)


def next_slot(tiles, lane):
    moved = [turned(t, -8) for t in tiles]
    return [jnp.where(lane >= 120, moved[(p + 1) % len(tiles)], moved[p]) for p in range(len(tiles))]


def last_slot(tiles, lane):
    moved = [turned(t, 8) for t in tiles]
    return [jnp.where(lane < 8, moved[p - 1], moved[p]) for p in range(len(tiles))]


def edge_depths(dp, side, rows):
    lane = lanes()
    tiles = []
    for part in range(len(rows) // 16):
        total = jnp.zeros((8, 128), F32)
        for s in range(16):
            near, beyond = depth_row(dp, rows[part * 16 + s] + GHOST, 3)[side], None
            beyond = depth_row(dp, rows[part * 16 + s] + GHOST, 3)[2]
            both = jnp.where(lane < 64, near, beyond) if side == 0 else jnp.where(lane < 64, beyond, near)
            total = jnp.where(lane // 8 == s, turned(both, 8 * s + 3), total)
        tiles.append(total)
    return tiles


def edge_coefs(side, parts, depths, eu, ev, ecoef, eck, edge_speed):
    lane = lanes()
    depth_e = [turned(d, -1) for d in depths]
    depth_n = next_slot(depths, lane)
    every = range(parts)
    for k in range(BANDS):
        at = pl.ds(8 * k, 8)
        level = level_of(k)
        us = [eu[side, p, at, :] for p in every]
        vs = [ev[side, p, at, :] for p in every]
        open_e = [level < jnp.minimum(depths[p], depth_e[p]) for p in every]
        open_n = [level < jnp.minimum(depths[p], depth_n[p]) for p in every]
        outs = [forth(us[p], open_e[p]) for p in every]
        backs = [back(us[p], open_e[p]) for p in every]
        norths = [forth(vs[p], open_n[p]) for p in every]
        souths = [back(vs[p], open_n[p]) for p in every]
        from_south, to_south = last_slot(norths, lane), last_slot(souths, lane)
        for p in every:
            down = jnp.where(level + 1.0 < depths[p], V_KAPPA, 0.0)
            upward = jnp.where(above_of(k) < depths[p], V_KAPPA, 0.0)
            flows = (outs[p] + turned(backs[p], 1)) + (norths[p] + to_south[p])
            ecoef[side, p, 0, at, :] = 1.0 - (flows + (down + upward))
            ecoef[side, p, 1, at, :] = backs[p]
            ecoef[side, p, 2, at, :] = turned(outs[p], 1)
            ecoef[side, p, 3, at, :] = souths[p]
            ecoef[side, p, 4, at, :] = from_south[p]
            eck[side, p, pl.ds(PAD + 8 * k, 8), :] = down
            if k == 0:
                eck[side, p, pl.ds(0, 8), :] = jnp.zeros((8, 128), F32)
            if side == 0:
                edge_speed[p, at, :] = jnp.where(open_e[p], us[p], SHUT)


def edge_step(parts, old, new, ecoef, eck):
    lane = lanes()

    def one(j, _):
        t = j // 2
        side = j % 2
        for k in range(BANDS):
            at = pl.ds(8 * k, 8)
            here = pl.ds(PAD + 8 * k, 8)
            above = pl.ds(PAD + 8 * k - 1, 8)
            below = pl.ds(PAD + 8 * k + 1, 8)
            tiles = [old[t, side, p, here, :] for p in range(parts)]
            north, south = next_slot(tiles, lane), last_slot(tiles, lane)
            for p in range(parts):
                c = [ecoef[side, p, n, at, :] for n in range(5)]
                total = c[0] * tiles[p] + c[1] * turned(tiles[p], -1) + c[2] * turned(tiles[p], 1)
                total += c[3] * north[p] + c[4] * south[p]
                total += eck[side, p, above, :] * old[t, side, p, above, :]
                total += eck[side, p, here, :] * old[t, side, p, below, :]
                new[t, side, p, here, :] = total
        return 0

    lax.fori_loop(0, 4, one, 0)


def edge_beside(parts, old, beside):
    lane = lanes()
    for t in range(2):
        for p in range(parts):
            for k in range(BANDS):
                here = pl.ds(PAD + 8 * k, 8)
                west, east = old[t, 0, p, here, :], old[t, 1, p, here, :]
                beside[t, p, pl.ds(8 * k, 8), :] = jnp.where(lane % 8 == 3, east, turned(west, 2))


def clear_levels(ref):
    zeros = jnp.zeros((8, 128), F32)
    for t in range(2):
        for side in range(2):
            for p in range(ref.shape[2]):
                ref[t, side, p, pl.ds(0, 8), :] = zeros
                ref[t, side, p, pl.ds(DEEP - 8, 8), :] = zeros


def faces_kernel(vp, dp, cr, ct, ck):
    def one(i, _):
        make_faces(i, vp, dp, cr, ct)
        make_column(i, dp, ck)
        return 0

    lax.fori_loop(GHOST, GHOST + ROWS, one, 0)


def corner_kernel(from_east, from_west, strip, dp_in, first_in, second_in, pe, dp, first, second):
    lane = lanes()
    strip_lane = lax.broadcasted_iota(jnp.int32, (ROWS, 128), 1)
    edge = pl.ds(8 * LEV, ROWS)
    dp[2, pl.ds(DROW, ROWS), :] = jnp.where(strip_lane < 64, from_east[edge, :], from_west[edge, :])
    for f in range(4):
        for part in range(2):
            for k in range(BANDS):
                at = pl.ds((f * 2 + part) * LEV + 8 * k, 8)
                mine = strip[at, :]
                pe[f, 0, part, pl.ds(8 * k, 8), :] = jnp.where(lane % 8 < 3, from_west[at, :], mine)
                pe[f, 1, part, pl.ds(8 * k, 8), :] = jnp.where(lane % 8 < 3, mine, from_east[at, :])

    def fill(out, north):
        part = jnp.where(north, 1, 0)
        for k in range(BANDS):
            total = jnp.zeros((8, 128), F32)
            for f in range(4):
                for side in range(2):
                    tile = pe[f, side, part, pl.ds(8 * k, 8), :]
                    for g in range(2):
                        n = f * 4 + side * 2 + g
                        moved = turned(tile, 8 * jnp.where(north, n - 15 + g, n - g))
                        total = jnp.where(lane // 8 == n, moved, total)
            out[pl.ds(CORNERS + 8 * k, 8), :] = total
        out[pl.ds(CORNERS + LEV, 16), :] = jnp.zeros((16, 128), F32)
        for i in range(3):
            r = jnp.where(north, ROWS - 1 - i, i)
            out[pl.ds(CORNERS + LEV + i, 1), :] = dp[2, pl.ds(r + DROW, 1), :]

    fill(first, is_even())
    fill(second, jnp.logical_not(is_even()))

    @pl.when(is_top())
    def _():
        place = lane % 8
        source = jnp.where(lane >= 96, (lane // 8 ^ 2) | 1, lane // 8 ^ 2)
        index = 8 * source + jnp.where(place < 6, 5 - place, place)
        for k in range(BANDS):
            at = pl.ds(CORNERS + 8 * k, 8)
            second[at, :] = gathered(second[at, :], index)
        at = pl.ds(CORNERS + LEV, 8)
        second[at, :] = gathered(second[at, :], 127 - lane)


def shift_row(row, k, old, beside, shifted):
    i, part, slot = row
    lane = lanes()
    here = pl.ds(PAD + 8 * k, 8)
    at = pl.ds(8 * k, 8)
    for t in range(2):
        left, right = old[t, i, 0, here, :], old[t, i, 1, here, :]
        outer = turned(beside[t, part, at, :], -8 * slot - 4)
        left_e, right_e = turned(left, -1), turned(right, -1)
        left_w, right_w = turned(left, 1), turned(right, 1)
        shifted[t, 0, at, :] = jnp.where(lane == 127, right_e, left_e)
        shifted[t, 1, at, :] = jnp.where(lane == 127, outer, right_e)
        shifted[t, 2, at, :] = jnp.where(lane == 0, outer, left_w)
        shifted[t, 3, at, :] = jnp.where(lane == 0, left_w, right_w)


def advance_row(i, k, old, new, shifted, cc, ce, cw, cr, ct, ck):
    at = pl.ds(8 * k, 8)
    here = pl.ds(PAD + 8 * k, 8)
    above = pl.ds(PAD + 8 * k - 1, 8)
    below = pl.ds(PAD + 8 * k + 1, 8)
    for n in range(2):
        c_c, c_e, c_w = cc[i, n, at, :], ce[i, n, at, :], cw[i, n, at, :]
        c_n, c_s = ct[i, n, at, :], cr[i - 1, n, at, :]
        c_d, c_u = ck[i, n, here, :], ck[i, n, above, :]
        for t in range(2):
            total = c_c * old[t, i, n, here, :]
            total += c_e * shifted[t, n, at, :] + c_w * shifted[t, 2 + n, at, :]
            total += c_n * old[t, i + 1, n, here, :] + c_s * old[t, i - 1, n, here, :]
            total += c_u * old[t, i, n, above, :] + c_d * old[t, i, n, below, :]
            new[t, i, n, here, :] = total


def send_rows(rows, new, result, sem):
    for i in rows:
        for half in range(2):
            pltpu.make_async_copy(
                new.at[:, i, half, pl.ds(PAD, LEV), :],
                result.at[:, :, i - GHOST, pl.ds(128 * half, 128)],
                sem,
            ).start()


def inner_kernel(
    x_in, up, dp, cr, ct, ck, pe,
    x, y, cc, ce, cw, result, shifted, e0, e1, ecoef, eck, edge_speed, beside, sem,
):
    coefs = (cc, ce, cw, cr, ct, ck)
    zeros = jnp.zeros((8, 128), F32)

    def clear(i, _):
        for t in range(2):
            for n in range(2):
                y[t, i, n, pl.ds(0, 8), :] = zeros
                y[t, i, n, pl.ds(DEEP - 8, 8), :] = zeros
        return 0

    lax.fori_loop(0, PLANES, clear, 0)

    rows = list(range(ROWS))
    clear_levels(e0)
    clear_levels(e1)
    for side in range(2):
        edge_coefs(side, 2, edge_depths(dp, side, rows), pe.at[2], pe.at[3], ecoef, eck, edge_speed)
        for t in range(2):
            for p in range(2):
                e0[t, side, p, pl.ds(PAD, LEV), :] = pe[t, side, p]

    def setup(i, _):
        planes = [GHOST + 1 + 2 * i + n for n in range(2)]
        placed = [(p, (p - GHOST) // 16, (p - GHOST) % 16) for p in planes]
        make_cells(placed, up, dp, edge_speed, *coefs)
        return 0

    lax.fori_loop(0, ROWS // 2 - 1, setup, 0)
    edge_beside(2, e0, beside.at[0])
    edge_step(2, e0, e1, ecoef, eck)
    edge_beside(2, e1, beside.at[1])
    edge_step(2, e1, e0, ecoef, eck)
    edge_beside(2, e0, beside.at[2])

    for step in range(3):
        old, new = (x, y) if step != 1 else (y, x)
        low = GHOST + 1 + step

        def placed(i):
            i = jnp.minimum(i, GHOST + ROWS - 1)
            return i, (i - GHOST) // 16, (i - GHOST) % 16

        for k in range(BANDS):
            shift_row(placed(low), k, old, beside.at[step], shifted.at[0])

        def body(j, _, low=low, old=old, new=new, step=step, placed=placed):
            i = low + 2 * j
            for n in range(2):
                for k in range(BANDS):
                    shift_row(placed(i + n + 1), k, old, beside.at[step], shifted.at[1 - n])
                    advance_row(i + n, k, old, new, shifted.at[n], *coefs)
            if step == 2:
                send_rows([i, i + 1], new, result, sem)
            return 0

        lax.fori_loop(0, (ROWS - 2 - 2 * step) // 2, body, 0)
    sent = y.at[:, pl.ds(2 * GHOST, ROWS - 2 * GHOST), :, pl.ds(PAD, LEV), :]
    pltpu.make_async_copy(sent, sent, sem).wait()


RIM_SOUTH = list(range(-GHOST, 5))
RIM_NORTH = list(range(ROWS - 5, ROWS + GHOST))


def rim_kernel(
    got_first, got_second,
    x_in, y_in, cc_in, ce_in, cw_in, cr_in, ct_in, ck_in, up_in, vp_in, dp_in, pe, result_in,
    x, y, cc, ce, cw, cr, ct, ck, up, vp, dp, result,
    shifted, e0, e1, eflow, ecoef, eck, edge_speed, beside, corners, sem,
):
    lane = lanes()
    coefs = (cc, ce, cw, cr, ct, ck)
    bottommost = lax.axis_index("lat") == 0

    def unpack(got, north, mirrored):
        corner = got.at[pl.ds(CORNERS, CORNER), :]

        def plane(i):
            return GHOST + ROWS + i if north else GHOST - 1 - i

        places = [(x.at[t], plane(i), PAD) for t in range(2) for i in range(3)]
        places += [(vp, plane(j - 1 if north else j), 0) for j in range(3)]
        places += [(up, plane(i), 0) for i in range(2)]
        for n, (ref, i, offset) in enumerate(places):
            if north and n == 6:
                continue
            for k in range(BANDS):
                at = pl.ds(offset + 8 * k, 8)
                tiles = [got[pl.ds((2 * n + half) * LEV + 8 * k, 8), :] for half in range(2)]
                if north and 6 <= n < 9:
                    tiles = [jnp.where(mirrored, -tile, tile) for tile in tiles]
                if north and n >= 9:
                    g = n - 9
                    beyond = turned(corner[pl.ds(8 * k, 8), :], -8 * (2 * 4 + 2 + g) - 3)
                    moved = [turned(tile, -1) for tile in tiles]
                    east = [
                        jnp.where(lane == 127, moved[1], moved[0]),
                        jnp.where(lane == 127, turned(beyond, -1), moved[1]),
                    ]
                    tiles = [jnp.where(mirrored, -b, a) for a, b in zip(tiles, east)]
                for half in range(2):
                    ref[i, half, at, :] = tiles[half]
        for i in range(3):
            at = pl.ds(plane(i) - GHOST + DROW, 1)
            rows = [got[pl.ds(DEPTHS + 2 * i + half, 1), :] for half in range(2)]
            rows.append(corner[pl.ds(LEV + i, 1), :])
            for third in range(3):
                dp[third, at, :] = rows[third] if north else jnp.where(bottommost, 0.0, rows[third])
        for k in range(BANDS):
            at = pl.ds(8 * k, 8)
            tile = corner[at, :]
            if north:
                west_face = -turned(tile, -1)
                changed = jnp.where(lane >= 96, -tile, jnp.where(lane >= 64, west_face, tile))
                tile = jnp.where(mirrored, changed, tile)
            corners[1 if north else 0, at, :] = tile

    @pl.when(is_even())
    def _():
        unpack(got_first, True, False)
        unpack(got_second, False, False)

    @pl.when(jnp.logical_not(is_even()))
    def _():
        unpack(got_second, True, is_top())
        unpack(got_first, False, False)

    clear_levels(e0)
    clear_levels(e1)
    for k in range(BANDS):
        at = pl.ds(8 * k, 8)
        south, north = corners[0, at, :], corners[1, at, :]
        for f in range(4):
            for side in range(2):
                low, high = turned(pe[f, side, 0, at, :], 24), turned(pe[f, side, 1, at, :], -24)
                total = jnp.where(lane < 64, low, high)
                total = jnp.where(jnp.logical_or(lane < 24, lane >= 104), 0.0, total)
                for g in range(2):
                    n = f * 4 + side * 2 + g
                    total = jnp.where(lane // 8 == 2 - g, turned(south, 8 * (2 - g - n)), total)
                    total = jnp.where(lane // 8 == 13 + g, turned(north, 8 * (13 + g - n)), total)
                if f < 2:
                    e0[f, side, 0, pl.ds(PAD + 8 * k, 8), :] = total
                else:
                    eflow[f - 2, side, 0, at, :] = total
    for side in range(2):
        depths = edge_depths(dp, side, RIM_SOUTH + RIM_NORTH)
        edge_coefs(side, 1, depths, eflow.at[0], eflow.at[1], ecoef, eck, edge_speed)
    edge_beside(1, e0, beside.at[0])
    edge_step(1, e0, e1, ecoef, eck)
    edge_beside(1, e1, beside.at[1])
    edge_step(1, e1, e0, ecoef, eck)
    edge_beside(1, e0, beside.at[2])

    south, north = GHOST, GHOST + ROWS

    for i in [south - 3 + j for j in range(3)] + [north - 1 + j for j in range(3)]:
        make_faces(i, vp, dp, cr, ct)
    for j in range(3):
        a, b = south - 2 + j, north - 1 + j
        for i in (a, b):
            make_column(i, dp, ck)
        make_cells([(a, 0, a), (b, 0, b - north + 13)], up, dp, edge_speed, *coefs)

    for step in range(3):
        old, new = (x, y) if step != 1 else (y, x)
        rows = []
        for j in range(3):
            a, b = south - 2 + step + j, north - 1 - step + j
            rows += [(a, 0, a), (b, 0, b - north + 13)]

        def shift(n, rows=rows, old=old, step=step):
            for k in range(BANDS):
                shift_row(rows[n], k, old, beside.at[step], shifted.at[n])

        shift(0)
        shift(1)
        for n in range(6):
            if n < 4:
                shift(n + 2)
            for k in range(BANDS):
                advance_row(rows[n][0], k, old, new, shifted.at[n], *coefs)
    for start in (south, north - GHOST):
        send_rows([start + n for n in range(3)], y, result, sem)
    sent = y.at[:, pl.ds(0, 2 * GHOST), :, pl.ds(PAD, LEV), :]
    pltpu.make_async_copy(sent, sent, sem).wait()


def shape(*dims):
    return jax.ShapeDtypeStruct(dims, F32)


def vmem(dims):
    return pltpu.VMEM(dims, F32)


def near(*arrays):
    return [pltpu.with_memory_space_constraint(array, pltpu.VMEM) for array in arrays]


def far(*arrays):
    return [pltpu.with_memory_space_constraint(array, pltpu.HBM) for array in arrays]


IN_VMEM = pl.BlockSpec(memory_space=pltpu.VMEM)
IN_HBM = pl.BlockSpec(memory_space=pltpu.HBM)
STATE = (2, PLANES, 2, DEEP, 128)
COEF = (PLANES, 2, LEV, 128)
COLUMN = (PLANES, 2, DEEP, 128)
DEPTH = (3, DROW + ROWS + 8, 128)
SHIFTED = (2, 4, LEV, 128)
EDGES = (4, 2, 2, LEV, 128)


def edge_scratch(parts):
    return [
        vmem((2, 2, parts, DEEP, 128)),
        vmem((2, 2, parts, DEEP, 128)),
        vmem((2, parts, 5, LEV, 128)),
        vmem((2, parts, DEEP, 128)),
        vmem((parts, LEV, 128)),
        vmem((3, 2, parts, LEV, 128)),
    ]


def call(kernel, args, outs, aliases=None, limit=4, **more):
    return pl.pallas_call(
        kernel,
        out_shape=outs,
        input_output_aliases=aliases or {},
        compiler_params=pltpu.CompilerParams(vmem_limit_bytes=limit << 20),
        **more,
    )(*args)


def cost(flops, moved):
    return pl.CostEstimate(flops=flops, bytes_accessed=moved, transcendentals=0)


def local(tracers, u_east, v_north, bottom):
    lon_size, lat_size = lax.axis_size("lon"), lax.axis_size("lat")
    inputs = (*far(tracers, u_east, v_north), bottom)
    x, up, vp, dp, strip = call(
        load_kernel,
        inputs,
        [vmem(STATE), vmem(COEF), vmem(COEF), vmem(DEPTH), shape(STRIP, 128)],
        in_specs=[IN_HBM] * 3 + [IN_VMEM],
        out_specs=[IN_VMEM] * 5,
        scratch_shapes=[pltpu.SemaphoreType.DMA((3,))],
        name="load",
    )
    eastward = [(i, (i + 1) % lon_size) for i in range(lon_size)]
    from_west = lax.ppermute(strip, "lon", eastward)
    from_east = lax.ppermute(strip, "lon", [(b, a) for a, b in eastward])
    first, second = call(
        rows_kernel,
        near(x, up, vp, dp),
        [vmem((PACKED, 128))] * 2,
        in_specs=[IN_VMEM] * 4,
        out_specs=[IN_VMEM] * 2,
        scratch_shapes=[pltpu.SemaphoreType.DMA((2,))],
        name="rows",
        cost_estimate=cost(1_000_000, 4_000_000),
    )
    cr, ct, ck = call(
        faces_kernel,
        near(vp, dp),
        [vmem(COEF), vmem(COEF), vmem(COLUMN)],
        in_specs=[IN_VMEM] * 2,
        out_specs=[IN_VMEM] * 3,
        name="faces",
        cost_estimate=cost(6_000_000, 8_000_000),
    )
    pe, dp, first, second = call(
        corner_kernel,
        (from_east, from_west, strip, *near(dp, first, second)),
        [vmem(EDGES), vmem(DEPTH), vmem((PACKED, 128)), vmem((PACKED, 128))],
        {3: 1, 4: 2, 5: 3},
        in_specs=[IN_VMEM] * 6,
        out_specs=[IN_VMEM] * 4,
        name="corner",
    )
    got_first = lax.ppermute(first, "lat", [(lat, lat ^ 1) for lat in range(lat_size)])
    pairs = []
    for lon in range(lon_size):
        pairs.append((lon * lat_size, (lon ^ 1) * lat_size))
        for lat in range(1, lat_size - 1):
            pairs.append((lon * lat_size + lat, lon * lat_size + (lat + 1 if lat % 2 else lat - 1)))
        pairs.append((lon * lat_size + lat_size - 1, (lon_size - 1 - lon) * lat_size + lat_size - 1))
    got_second = lax.ppermute(second, ("lon", "lat"), pairs)

    x, y, cc, ce, cw, result = call(
        inner_kernel,
        near(x, up, dp, cr, ct, ck, pe),
        [vmem(STATE), vmem(STATE)] + [vmem(COEF)] * 3 + [shape(*tracers.shape)],
        {0: 0},
        limit=16,
        in_specs=[IN_VMEM] * 7,
        out_specs=[IN_VMEM] * 5 + [IN_HBM],
        scratch_shapes=[vmem((2, *SHIFTED)), *edge_scratch(2), pltpu.SemaphoreType.DMA(())],
        name="inner",
        cost_estimate=cost(60_000_000, 20_000_000),
    )
    held = [x, y, cc, ce, cw, cr, ct, ck, up, vp, dp]
    sizes = [STATE, STATE] + [COEF] * 5 + [COLUMN, COEF, COEF, DEPTH]
    edge_lists = edge_scratch(1)
    return call(
        rim_kernel,
        (got_first, got_second, *near(*held, pe), *far(result)),
        [vmem(s) for s in sizes] + [shape(*tracers.shape)],
        {2 + n: n for n in range(11)} | {14: 11},
        limit=16,
        in_specs=[IN_VMEM] * 14 + [IN_HBM],
        out_specs=[IN_VMEM] * 11 + [IN_HBM],
        scratch_shapes=[
            vmem((6, *SHIFTED)), *edge_lists[:2], vmem((2, 2, 1, LEV, 128)), *edge_lists[2:],
            vmem((2, LEV, 128)), pltpu.SemaphoreType.DMA(()),
        ],
        name="rim",
    )[-1]


def solution(mesh):
    placed = (
        P(None, None, "lat", "lon"),
        P(None, "lat", "lon"),
        P(None, "lat", "lon"),
        P("lat", "lon"),
    )
    return jax.shard_map(
        local, mesh=mesh, in_specs=placed, out_specs=P(None, None, "lat", "lon"), check_vma=False
    )
```

profile of v0, /device:TPU:7, one launch (start us, length us, event | category | flops | bytes accessed | tf_op | source)
XLA Modules:
  0.0 39.6 jit_solution(9416462560321962491)
XLA Ops:
  0.0 0.0 copy-start
  0.0 0.8 %copy-done = s32[32,256]{1,0:T(8,128)S(1)} copy-done((s32[32,256]{1,0:T(8,128)S(1)}, s32[32,256]{1,0:T(8,128)}, u32[]{:S(2)}) %copy-start) | copy-done | bytes 32792
  0.8 4.9 %load.1 = (f32[2,38,2,64,128]{4,3,2,1,0:T(8,128)S(1)}, f32[38,2,48,128]{3,2,1,0:T(8,128)S(1)}, f32[38,2,48,128]{3,2,1,0:T(8,128)S(1)}, f32[3,48,128]{2,1,0:T(8,128)S(1)}, f32[416,128]{1,0:T(8,128)S(1)}) custom-call(f32[2,48,32,256]{3,2,1,0:T(8,128)} %tr.1, f32[48,32,256]{2,1,0:T(8,128)} %u.1, f32[48,32,256]{2,1,0:T(8,128)} %v.1, s32[32,256]{1,0:T(8,128)S(1)} %copy-done), custom_call_target="tpu_custom_call" | custom-call | tf_op jit(solution)/shard_map/load/pallas_call | solution.py:671
  5.7 2.2 %collective-permute-start.1 = (f32[416,128]{1,0:T(8,128)S(1)}, f32[416,128]{1,0:T(8,128)S(1)}, u32[]{:S(2)}, u32[]{:S(2)}) collective-permute-start(f32[416,128]{1,0:T(8,128)S(1)} %get-tuple-element.26.strip), channel_id=1, source_target_pairs={{0,8},{8,16},{16,24},{24,32},{32,40},{40,48},{48,56},{56,64},{64,7... | collective-permute-start | bytes 638984 | tf_op jit(solution)/shard_map/ppermute | solution.py:697
  7.9 0.0 collective-permute-start
  7.9 1.4 %rows.1 = (f32[1136,128]{1,0:T(8,128)S(1)}, f32[1136,128]{1,0:T(8,128)S(1)}) custom-call(f32[2,38,2,64,128]{4,3,2,1,0:T(8,128)S(1)} %get-tuple-element.28.x.x_in, f32[38,2,48,128]{3,2,1,0:T(8,128)S(1)} %get-tuple-element.29.up.up_in, f32[38,2,48,128]{3,2,1,0:T(8,128)S(1)} %get-tuple-element.30.vp.vp_in, f32[3,48,128]{2,1,0:T(8,128)S(1)} %get-tuple-element.27.dp.dp_in), custom_call_target="tpu_custom_call" | custom-call | flops 1000000 | bytes 4000000 | tf_op jit(solution)/shard_map/rows/pallas_call | solution.py:671
  9.3 0.6 %faces.1 = (f32[38,2,48,128]{3,2,1,0:T(8,128)S(1)}, f32[38,2,48,128]{3,2,1,0:T(8,128)S(1)}, f32[38,2,64,128]{3,2,1,0:T(8,128)S(1)}) custom-call(f32[38,2,48,128]{3,2,1,0:T(8,128)S(1)} %get-tuple-element.30.vp.vp_in, f32[3,48,128]{2,1,0:T(8,128)S(1)} %get-tuple-element.27.dp.dp_in), custom_call_target="tpu_custom_call" | custom-call | flops 6000000 | bytes 8000000 | tf_op jit(solution)/shard_map/faces/pallas_call | solution.py:671
  10.0 2.6 %collective-permute-done.1.from_west = f32[416,128]{1,0:T(8,128)S(1)} collective-permute-done((f32[416,128]{1,0:T(8,128)S(1)}, f32[416,128]{1,0:T(8,128)S(1)}, u32[]{:S(2)}, u32[]{:S(2)}) %collective-permute-start.1) | collective-permute-done | bytes 213024 | tf_op jit(solution)/shard_map/ppermute | solution.py:697
  12.5 1.8 %collective-permute-done.from_east = f32[416,128]{1,0:T(8,128)S(1)} collective-permute-done((f32[416,128]{1,0:T(8,128)S(1)}, f32[416,128]{1,0:T(8,128)S(1)}, u32[]{:S(2)}, u32[]{:S(2)}) %collective-permute-start) | collective-permute-done | bytes 213024 | tf_op jit(solution)/shard_map/ppermute | solution.py:698
  14.3 0.3 corner.1
  14.6 1.7 %collective-permute-start.2 = (f32[1136,128]{1,0:T(8,128)S(1)}, f32[1136,128]{1,0:T(8,128)S(1)}, u32[]{:S(2)}, u32[]{:S(2)}) collective-permute-start(f32[1136,128]{1,0:T(8,128)S(1)} %get-tuple-element.33), channel_id=1, source_target_pairs={{0,1},{1,0},{2,3},{3,2},{4,5},{5,4},{6,7},{7,6},{8,9},{9,8},{10,11... | collective-permute-start | bytes 1744904 | tf_op jit(solution)/shard_map/ppermute | solution.py:727
  16.4 3.1 %collective-permute-start.3 = (f32[1136,128]{1,0:T(8,128)S(1)}, f32[1136,128]{1,0:T(8,128)S(1)}, u32[]{:S(2)}, u32[]{:S(2)}) collective-permute-start(f32[1136,128]{1,0:T(8,128)S(1)} %get-tuple-element.34), channel_id=1, source_target_pairs={{0,8},{1,2},{2,1},{3,4},{4,3},{5,6},{6,5},{7,127},{8,0},{9,10},{10... | collective-permute-start | bytes 1744904 | tf_op jit(solution)/shard_map/ppermute | solution.py:734
  19.4 16.1 %inner.1 = (f32[2,38,2,64,128]{4,3,2,1,0:T(8,128)S(1)}, f32[2,38,2,64,128]{4,3,2,1,0:T(8,128)S(1)}, f32[38,2,48,128]{3,2,1,0:T(8,128)S(1)}, f32[38,2,48,128]{3,2...) custom-call(f32[2,38,2,64,128]{4,3,2,1,0:T(8,128)S(1)} %get-tuple-el, ...), custom_call_target="tpu_custom_call", output_to_operand_aliasing={{0}: (0, {})} | custom-call | flops 60000000 | bytes 20000000 | tf_op jit(solution)/shard_map/inner/pallas_call | solution.py:671
  35.6 0.0 collective-permute-done.2.got_first
  35.6 0.0 collective-permute-done.3.got_second
  35.6 4.0 %rim.1 = (f32[2,38,2,64,128]{4,3,2,1,0:T(8,128)S(1)}, f32[2,38,2,64,128]{4,3,2,1,0:T(8,128)S(1)}, f32[38,2,48,128]{3,2,1,0:T(8,128)S(1)}, f32[38,2,48,128]{3,2,1...) custom-call(f32[1136,128]{1,0:T(8,128)S(1)} %collective-permute-done, ...), custom_call_target="tpu_custom_call", output_to_operand_aliasing={{0}: (2, {}), {1}: (3, {}), {2}: (4, {}), {3}: (5, {}), {4}... | custom-call | tf_op jit(solution)/shard_map/rim/pallas_call | solution.py:671
Async XLA Ops:
  0.0 0.8 %copy-start = (s32[32,256]{1,0:T(8,128)S(1)}, s32[32,256]{1,0:T(8,128)}, u32[]{:S(2)}) copy-start(s32[32,256]{1,0:T(8,128)} %bottom.1) | copy-start | bytes 98308
  5.7 6.9 %collective-permute-start.1 = (f32[416,128]{1,0:T(8,128)S(1)}, f32[416,128]{1,0:T(8,128)S(1)}, u32[]{:S(2)}, u32[]{:S(2)}) collective-permute-start(f32[416,128]{1,0:T(8,128)S(1)} %get-tuple-element.26.strip), channel_id=1, source_target_pairs={{0,8},{8,16},{16,24},{24,32},{32,40},{40,48},{48,56},{56,64},{64,7... | collective-permute-start | bytes 638984 | tf_op jit(solution)/shard_map/ppermute | solution.py:697
  7.9 6.4 %collective-permute-start = (f32[416,128]{1,0:T(8,128)S(1)}, f32[416,128]{1,0:T(8,128)S(1)}, u32[]{:S(2)}, u32[]{:S(2)}) collective-permute-start(f32[416,128]{1,0:T(8,128)S(1)} %get-tuple-element.26.strip), channel_id=1, source_target_pairs={{8,0},{16,8},{24,16},{32,24},{40,32},{48,40},{56,48},{64,56},{72,6... | collective-permute-start | bytes 638984 | tf_op jit(solution)/shard_map/ppermute | solution.py:698
  14.6 20.9 %collective-permute-start.2 = (f32[1136,128]{1,0:T(8,128)S(1)}, f32[1136,128]{1,0:T(8,128)S(1)}, u32[]{:S(2)}, u32[]{:S(2)}) collective-permute-start(f32[1136,128]{1,0:T(8,128)S(1)} %get-tuple-element.33), channel_id=1, source_target_pairs={{0,1},{1,0},{2,3},{3,2},{4,5},{5,4},{6,7},{7,6},{8,9},{9,8},{10,11... | collective-permute-start | bytes 1744904 | tf_op jit(solution)/shard_map/ppermute | solution.py:727
  16.4 19.2 %collective-permute-start.3 = (f32[1136,128]{1,0:T(8,128)S(1)}, f32[1136,128]{1,0:T(8,128)S(1)}, u32[]{:S(2)}, u32[]{:S(2)}) collective-permute-start(f32[1136,128]{1,0:T(8,128)S(1)} %get-tuple-element.34), channel_id=1, source_target_pairs={{0,8},{1,2},{2,1},{3,4},{4,3},{5,6},{6,5},{7,127},{8,0},{9,10},{10... | collective-permute-start | bytes 1744904 | tf_op jit(solution)/shard_map/ppermute | solution.py:734
where the time goes:
time: 39.8 us; the launch traced here: 39.6 us
  Pallas kernels  27.4 us (69%)
  starting transfers between devices  7 us (18%)
  waiting for transfers between devices  4.34 us (11%)
  local copies, waits for them, and re-layouts  0.76 us (2%)
    pallas_call x6, Pallas kernels, call(): pl.pallas_call(kernel, out_shape=outs, input_output_aliases=aliases or {}...  27.4 us
    ppermute x1, starting transfers between devices, local(): got_second = lax.ppermute(second, ('lon', 'lat'), pairs)  3.09 us
    ppermute x1, waiting for transfers between devices, local(): from_west = lax.ppermute(strip, 'lon', eastward)  2.57 us
    ppermute x1, starting transfers between devices, local(): from_west = lax.ppermute(strip, 'lon', eastward)  2.19 us
    ppermute x1, waiting for transfers between devices, local(): from_east = lax.ppermute(strip, 'lon', [(b, a) for a, b in eastward])  1.76 us
    ppermute x1, starting transfers between devices, local(): lax.ppermute(first, 'lat', [(lat, lat ^ 1) for lat in range(lat_size)])  1.72 us
  transfers between devices with their start and end apart: 4, of which 2 were waited for; matrix products, arithmetic and copies ran while one was open for 0% of the time, Pallas kernels for 46%

commit v1 on v0

--- a/solution.py
+++ b/solution.py
@@ -16,12 +16,14 @@
 PAD = 8
 DEEP = 64
 DROW = 8
-ITEMS = 11
+COPIED = 7
+ITEMS = COPIED + 2
 DEPTHS = ITEMS * 2 * LEV
 CORNERS = DEPTHS + 16
 CORNER = LEV + 16
 PACKED = CORNERS + CORNER
-STRIP = 4 * 2 * LEV + ROWS
+STRIP = 4 * 2 * LEV
+SENT = 4 * LEV + ROWS
 H_KAPPA = 0.06
 V_KAPPA = 0.08
 SHUT = 1e30
@@ -48,7 +50,17 @@
     return lax.axis_index("lat") % 2 == 0
 
 
-def rows_kernel(x, up, vp, dp, first, second, sems):
+def mirror(out, n):
+    back = 127 - lanes()
+    for k in range(BANDS):
+        a = pl.ds(2 * n * LEV + 8 * k, 8)
+        b = pl.ds((2 * n + 1) * LEV + 8 * k, 8)
+        left, right = out[a, :], out[b, :]
+        out[a, :] = gathered(right, back)
+        out[b, :] = gathered(left, back)
+
+
+def row_copies(x, up, vp, dp, first, second, sems):
     even = is_even()
 
     def fill(out, north, sem):
@@ -56,10 +68,10 @@
             return jnp.where(north, ROWS - 1 - i, i) + GHOST
 
         def face(j):
-            return jnp.where(north, ROWS - 1 - j, max(j - 1, 0)) + GHOST
-
-        items = [(x.at[t], row(i), PAD) for t in range(2) for i in range(3)]
-        items += [(vp, face(j), 0) for j in range(3)] + [(up, row(i), 0) for i in range(2)]
+            return jnp.where(north, ROWS - 1 - j, 0) + GHOST
+
+        items = [(x.at[t], row(i), PAD) for t in range(2) for i in range(2)]
+        items += [(vp, face(0), 0), (vp, face(1), 0), (up, row(0), 0)]
         for n, (ref, i, offset) in enumerate(items):
             for half in range(2):
                 pltpu.make_async_copy(
@@ -69,7 +81,7 @@
                 ).start()
 
     def finish(out, north, sem):
-        all_items = out.at[pl.ds(0, DEPTHS), :]
+        all_items = out.at[pl.ds(0, COPIED * 2 * LEV), :]
         pltpu.make_async_copy(all_items, all_items, sem).wait()
         out[pl.ds(DEPTHS, 16), :] = jnp.zeros((16, 128), F32)
         for i in range(3):
@@ -80,56 +92,54 @@
     odd = jnp.logical_not(even)
     fill(first, even, sems.at[0])
     fill(second, odd, sems.at[1])
-    finish(first, even, sems.at[0])
-    finish(second, odd, sems.at[1])
-
-    @pl.when(is_top())
-    def _():
-        back = 127 - lanes()
-
-        def turn(n, _):
-            for k in range(BANDS):
-                a = pl.ds(2 * n * LEV + 8 * k, 8)
-                b = pl.ds((2 * n + 1) * LEV + 8 * k, 8)
-                left, right = second[a, :], second[b, :]
-                second[a, :] = gathered(right, back)
-                second[b, :] = gathered(left, back)
-            return 0
-
-        lax.fori_loop(0, ITEMS, turn, 0)
-        rows = gathered(second[pl.ds(DEPTHS, 8), :], back)
-        for i in range(3):
+    def end():
+        finish(first, even, sems.at[0])
+        finish(second, odd, sems.at[1])
+
+        @pl.when(is_top())
+        def _():
+            back = 127 - lanes()
+
+            def turn(n, _):
+                mirror(second, n)
+                return 0
+
+            lax.fori_loop(0, COPIED, turn, 0)
+            rows = gathered(second[pl.ds(DEPTHS, 8), :], back)
+            for i in range(3):
+                for half in range(2):
+                    source = 2 * i + 1 - half
+                    second[pl.ds(DEPTHS + 2 * i + half, 1), :] = rows[source : source + 1, :]
+
+    return end
+
+
+def load_kernel(tr, u, v, bottom, x, up, vp, dp, strip, to_west, to_east, wet, sems):
+    wet_copy = pltpu.make_async_copy(bottom, wet, sems.at[3])
+    wet_copy.start()
+    for source, into, sem in ((u, up, sems.at[1]), (v, vp, sems.at[2])):
+        for r in range(ROWS):
             for half in range(2):
-                source = 2 * i + 1 - half
-                second[pl.ds(DEPTHS + 2 * i + half, 1), :] = rows[source : source + 1, :]
-
-
-def load_kernel(tr, u, v, bottom, x, up, vp, dp, strip, sems):
-    def start(r, _):
-        for half in range(2):
-            columns = pl.ds(128 * half, 128)
-            pltpu.make_async_copy(
-                tr.at[:, :, r, columns], x.at[:, r + GHOST, half, pl.ds(PAD, LEV), :], sems.at[0]
-            ).start()
-        return 0
-
-    def start_flow(r, _, source=None, into=None, sem=None):
+                columns = pl.ds(128 * half, 128)
+                pltpu.make_async_copy(source.at[:, r, columns], into.at[r + GHOST, half], sem).start()
+
+    def start_tracers(r):
         for half in range(2):
             pltpu.make_async_copy(
-                source.at[:, r, pl.ds(128 * half, 128)], into.at[r + GHOST, half], sem
+                tr.at[:, :, r, pl.ds(128 * half, 128)],
+                x.at[:, r + GHOST, half, pl.ds(PAD, LEV), :],
+                sems.at[0],
             ).start()
-        return 0
-
-    lax.fori_loop(0, ROWS, functools.partial(start_flow, source=u, into=up, sem=sems.at[1]), 0)
-    lax.fori_loop(0, ROWS, functools.partial(start_flow, source=v, into=vp, sem=sems.at[2]), 0)
-    lax.fori_loop(0, ROWS, start, 0)
-
-    depth = bottom[...].astype(F32)
+
+    wet_copy.wait()
+    depth = wet[...].astype(F32)
     dp[...] = jnp.zeros_like(dp)
     for half in range(2):
         dp[half, pl.ds(DROW, ROWS), :] = depth[:, 128 * half : 128 * half + 128]
     strip_lane = lax.broadcasted_iota(jnp.int32, (ROWS, 128), 1)
-    strip[pl.ds(8 * LEV, ROWS), :] = jnp.where(strip_lane < 64, depth[:, :128], depth[:, 128:])
+    edges = jnp.where(strip_lane < 64, depth[:, :128], depth[:, 128:])
+    to_west[pl.ds(4 * LEV, ROWS), :] = edges
+    to_east[pl.ds(4 * LEV, ROWS), :] = edges
 
     zeros = jnp.zeros((8, 128), F32)
     lane = lanes()
@@ -143,18 +153,35 @@
 
     lax.fori_loop(0, PLANES, clear, 0)
 
-    def pack(f, load):
-        def one(k, _):
-            for part in range(2):
-                total = zeros
-                for s in range(16):
-                    a, b = load(part * 16 + s + GHOST, k)
-                    both = turned(jnp.where(lane < 64, a, b), 8 * s + 3)
-                    total = jnp.where(lane // 8 == s, both, total)
-                strip[pl.ds((f * 2 + part) * LEV + 8 * k, 8), :] = total
+    def pack(f, load, starting=False):
+        def one(j, _):
+            for n in range(2):
+                k = 2 * j + n
+                halves = []
+                for part in range(2):
+                    total = zeros
+                    for s in range(16):
+                        if starting and s % 6 == 0:
+                            r = (k * 2 + part) * 3 + s // 6
+                            if r < ROWS:
+                                start_tracers(r)
+                        a, b = load(part * 16 + s + GHOST, k)
+                        both = turned(jnp.where(lane < 64, a, b), 8 * s + 3)
+                        total = jnp.where(lane // 8 == s, both, total)
+                    strip[pl.ds((f * 2 + part) * LEV + 8 * k, 8), :] = total
+                    halves.append(total)
+                at = pl.ds(f * LEV + 8 * k, 8)
+                to_west[at, :] = jnp.where(lane % 8 < 3, turned(halves[1], -3), halves[0])
+                to_east[at, :] = jnp.where(lane % 8 < 3, halves[0], turned(halves[1], 3))
             return 0
 
-        lax.fori_loop(0, BANDS, one, 0)
+        if starting:
+            for r in range(BANDS * 6, ROWS):
+                start_tracers(r)
+            for j in range(BANDS // 2):
+                one(j, 0)
+        else:
+            lax.fori_loop(0, BANDS // 2, one, 0)
 
     own = pl.ds(GHOST, ROWS)
     for n, ref in ((1, up), (2, vp)):
@@ -166,7 +193,7 @@
                 for half in range(2):
                     vp[GHOST + ROWS - 1, half] = jnp.zeros((LEV, 128), F32)
 
-        pack(n + 1, lambda i, k, ref=ref: [ref[i, half, pl.ds(8 * k, 8), :] for half in range(2)])
+        pack(n + 1, lambda i, k, ref=ref: [ref[i, half, pl.ds(8 * k, 8), :] for half in range(2)], n == 1)
     whole = x.at[:, own, :, pl.ds(PAD, LEV), :]
     pltpu.make_async_copy(whole, whole, sems.at[0]).wait()
     for t in range(2):
@@ -227,7 +254,7 @@
         for (i, part, slot), least in zip(rows, leasts):
             speeds = [jnp.where(level_of(k) < least[n], up[i, n, at, :], SHUT) for n in range(2)]
             a, b = [turned(speed, 1) for speed in speeds]
-            outer = turned(edge_speed[part, at, :], -8 * slot - 2)
+            outer = a if edge_speed is None else turned(edge_speed[part, at, :], -8 * slot - 2)
             wests = [jnp.where(lane == 0, outer, a), jnp.where(lane == 0, a, b)]
             for n in range(2):
                 open_e, open_w = speeds[n] < SHUT, wests[n] < SHUT
@@ -341,27 +368,52 @@
                 ref[t, side, p, pl.ds(DEEP - 8, 8), :] = zeros
 
 
-def faces_kernel(vp, dp, cr, ct, ck):
-    def one(i, _):
-        make_faces(i, vp, dp, cr, ct)
-        make_column(i, dp, ck)
+def early_kernel(x, up, vp, dp, cc, ce, cw, cr, ct, ck, beside, first, second, sems):
+    end = row_copies(x, up, vp, dp, first, second, sems)
+    lane = lanes()
+
+    def one(j, _):
+        for n in range(2):
+            r = 2 * j + n
+            i = r + GHOST
+            make_faces(i, vp, dp, cr, ct)
+            make_column(i, dp, ck)
+            make_cells([(i, 0, 0)], up, dp, None, cc, ce, cw, cr, ct, ck)
+            for k in range(BANDS):
+                at = pl.ds(8 * k, 8)
+                here = pl.ds(PAD + 8 * k, 8)
+                for t in range(2):
+                    left, right = x[t, i, 0, here, :], x[t, i, 1, here, :]
+                    right_e, left_w = turned(right, -1), turned(left, 1)
+                    beside[r, t, 0, at, :] = jnp.where(lane == 127, right_e, turned(left, -1))
+                    beside[r, t, 1, at, :] = right_e
+                    beside[r, t, 2, at, :] = left_w
+                    beside[r, t, 3, at, :] = jnp.where(lane == 0, left_w, turned(right, 1))
         return 0
 
-    lax.fori_loop(GHOST, GHOST + ROWS, one, 0)
-
-
-def corner_kernel(from_east, from_west, strip, dp_in, first_in, second_in, pe, dp, first, second):
-    lane = lanes()
+    lax.fori_loop(0, ROWS // 2, one, 0)
+    end()
+
+
+def corner_kernel(
+    from_east, from_west, strip, x, ahead, cr, ct, ck, dp_in, first_in, second_in, cc_in, ce_in, cw_in,
+    dp, first, second, cc, ce, cw, pe, y, e0, ecoef, eck, patch, beside, edge_speed,
+):
+    lane = lanes()
+    zeros = jnp.zeros((8, 128), F32)
     strip_lane = lax.broadcasted_iota(jnp.int32, (ROWS, 128), 1)
-    edge = pl.ds(8 * LEV, ROWS)
+    edge = pl.ds(4 * LEV, ROWS)
     dp[2, pl.ds(DROW, ROWS), :] = jnp.where(strip_lane < 64, from_east[edge, :], from_west[edge, :])
+    outer = lane % 8 < 3
     for f in range(4):
-        for part in range(2):
-            for k in range(BANDS):
-                at = pl.ds((f * 2 + part) * LEV + 8 * k, 8)
-                mine = strip[at, :]
-                pe[f, 0, part, pl.ds(8 * k, 8), :] = jnp.where(lane % 8 < 3, from_west[at, :], mine)
-                pe[f, 1, part, pl.ds(8 * k, 8), :] = jnp.where(lane % 8 < 3, mine, from_east[at, :])
+        for k in range(BANDS):
+            at = pl.ds(f * LEV + 8 * k, 8)
+            to = pl.ds(8 * k, 8)
+            west, east = from_west[at, :], from_east[at, :]
+            for part in range(2):
+                mine = strip[pl.ds((f * 2 + part) * LEV + 8 * k, 8), :]
+                pe[f, 0, part, to, :] = jnp.where(outer, turned(west, -3) if part else west, mine)
+                pe[f, 1, part, to, :] = jnp.where(outer, mine, turned(east, 3) if part else east)
 
     def fill(out, north):
         part = jnp.where(north, 1, 0)
@@ -383,8 +435,43 @@
     fill(first, is_even())
     fill(second, jnp.logical_not(is_even()))
 
+    def clear(i, _):
+        for t in range(2):
+            for n in range(2):
+                y[t, i, n, pl.ds(0, 8), :] = zeros
+                y[t, i, n, pl.ds(DEEP - 8, 8), :] = zeros
+        return 0
+
+    lax.fori_loop(0, PLANES, clear, 0)
+    clear_levels(e0)
+    for side in range(2):
+        depths = edge_depths(dp, side, list(range(ROWS)))
+        edge_coefs(side, 2, depths, pe.at[2], pe.at[3], ecoef, eck, edge_speed)
+        for t in range(2):
+            for p in range(2):
+                e0[t, side, p, pl.ds(PAD, LEV), :] = pe[t, side, p]
+    for p in range(2):
+        for k in range(BANDS):
+            at = pl.ds(8 * k, 8)
+            last = lane % 8 == 2
+            patch[0, p, at, :] = jnp.where(last, ecoef[1, p, 0, at, :], ecoef[0, p, 0, at, :])
+            patch[1, p, at, :] = jnp.where(last, ecoef[1, p, 1, at, :], ecoef[0, p, 2, at, :])
+    edge_beside(2, e0, beside)
+    near_south, near_north = GHOST + 1, GHOST + ROWS - 2
+    for k in range(BANDS):
+        for row in ((near_south, 0, 1), (near_north, 1, 14)):
+            first_row(row, k, x, y, ahead, beside, patch, cc, ce, cw, cr, ct, ck)
+    for out, north in ((first, is_even()), (second, jnp.logical_not(is_even()))):
+        i = jnp.where(north, near_north, near_south)
+        for t in range(2):
+            for half in range(2):
+                at = pl.ds((2 * (COPIED + t) + half) * LEV, LEV)
+                out[at, :] = y[t, i, half, pl.ds(PAD, LEV), :]
+
     @pl.when(is_top())
     def _():
+        mirror(second, COPIED)
+        mirror(second, COPIED + 1)
         place = lane % 8
         source = jnp.where(lane >= 96, (lane // 8 ^ 2) | 1, lane // 8 ^ 2)
         index = 8 * source + jnp.where(place < 6, 5 - place, place)
@@ -438,66 +525,88 @@
             ).start()
 
 
+def first_row(row, k, old, new, ahead, beside, patch, cc, ce, cw, cr, ct, ck):
+    i, part, slot = row
+    lane = lanes()
+    at = pl.ds(8 * k, 8)
+    here = pl.ds(PAD + 8 * k, 8)
+    above = pl.ds(PAD + 8 * k - 1, 8)
+    below = pl.ds(PAD + 8 * k + 1, 8)
+    edge = [lane == 0, lane == 127]
+    centre = turned(patch[0, part, at, :], -8 * slot - 3)
+    sides = turned(patch[1, part, at, :], -8 * slot - 3)
+    outer = [turned(beside[t, part, at, :], -8 * slot - 4) for t in range(2)]
+    for n in range(2):
+        c_c = jnp.where(edge[n], centre, cc[i, n, at, :])
+        cc[i, n, at, :] = c_c
+        c_e, c_w = ce[i, n, at, :], cw[i, n, at, :]
+        if n == 0:
+            c_w = jnp.where(edge[0], sides, c_w)
+            cw[i, n, at, :] = c_w
+        else:
+            c_e = jnp.where(edge[1], sides, c_e)
+            ce[i, n, at, :] = c_e
+        c_n, c_s = ct[i, n, at, :], cr[i - 1, n, at, :]
+        c_d, c_u = ck[i, n, here, :], ck[i, n, above, :]
+        for t in range(2):
+            east, west = ahead[i - GHOST, t, n, at, :], ahead[i - GHOST, t, 2 + n, at, :]
+            if n == 0:
+                west = jnp.where(edge[0], outer[t], west)
+            else:
+                east = jnp.where(edge[1], outer[t], east)
+            total = c_c * old[t, i, n, here, :] + c_e * east + c_w * west
+            total += c_n * old[t, i + 1, n, here, :] + c_s * old[t, i - 1, n, here, :]
+            total += c_u * old[t, i, n, above, :] + c_d * old[t, i, n, below, :]
+            new[t, i, n, here, :] = total
+
+
 def inner_kernel(
-    x_in, up, dp, cr, ct, ck, pe,
-    x, y, cc, ce, cw, result, shifted, e0, e1, ecoef, eck, edge_speed, beside, sem,
+    x_in, y_in, cc_in, ce_in, cw_in, cr, ct, ck, e0_in, ecoef, eck, patch, ahead, beside_in,
+    x, y, cc, ce, cw, result, e0, shifted, e1, beside, sem,
 ):
     coefs = (cc, ce, cw, cr, ct, ck)
-    zeros = jnp.zeros((8, 128), F32)
-
-    def clear(i, _):
-        for t in range(2):
-            for n in range(2):
-                y[t, i, n, pl.ds(0, 8), :] = zeros
-                y[t, i, n, pl.ds(DEEP - 8, 8), :] = zeros
+
+    def placed(i):
+        i = jnp.minimum(i, GHOST + ROWS - 1)
+        return i, (i - GHOST) // 16, (i - GHOST) % 16
+
+    def first(j, _):
+        for n in range(2):
+            for k in range(BANDS):
+                first_row(placed(GHOST + 2 + 2 * j + n), k, x, y, ahead, beside_in, patch, *coefs)
         return 0
 
-    lax.fori_loop(0, PLANES, clear, 0)
-
-    rows = list(range(ROWS))
-    clear_levels(e0)
+    lax.fori_loop(0, ROWS // 2 - 2, first, 0)
     clear_levels(e1)
-    for side in range(2):
-        edge_coefs(side, 2, edge_depths(dp, side, rows), pe.at[2], pe.at[3], ecoef, eck, edge_speed)
-        for t in range(2):
-            for p in range(2):
-                e0[t, side, p, pl.ds(PAD, LEV), :] = pe[t, side, p]
-
-    def setup(i, _):
-        planes = [GHOST + 1 + 2 * i + n for n in range(2)]
-        placed = [(p, (p - GHOST) // 16, (p - GHOST) % 16) for p in planes]
-        make_cells(placed, up, dp, edge_speed, *coefs)
-        return 0
-
-    lax.fori_loop(0, ROWS // 2 - 1, setup, 0)
-    edge_beside(2, e0, beside.at[0])
     edge_step(2, e0, e1, ecoef, eck)
-    edge_beside(2, e1, beside.at[1])
+    edge_beside(2, e1, beside.at[0])
     edge_step(2, e1, e0, ecoef, eck)
-    edge_beside(2, e0, beside.at[2])
-
-    for step in range(3):
+    edge_beside(2, e0, beside.at[1])
+
+    for step in range(1, 3):
         old, new = (x, y) if step != 1 else (y, x)
         low = GHOST + 1 + step
-
-        def placed(i):
-            i = jnp.minimum(i, GHOST + ROWS - 1)
-            return i, (i - GHOST) // 16, (i - GHOST) % 16
-
-        for k in range(BANDS):
-            shift_row(placed(low), k, old, beside.at[step], shifted.at[0])
-
-        def body(j, _, low=low, old=old, new=new, step=step, placed=placed):
-            i = low + 2 * j
-            for n in range(2):
+        count = ROWS - 2 - 2 * step
+        for n in range(2):
+            for k in range(BANDS):
+                shift_row(placed(low + n), k, old, beside.at[step - 1], shifted.at[n])
+
+        def body(j, _, low=low, old=old, new=new, step=step):
+            i = low + 4 * j
+            for n in range(4):
                 for k in range(BANDS):
-                    shift_row(placed(i + n + 1), k, old, beside.at[step], shifted.at[1 - n])
+                    shift_row(placed(i + n + 2), k, old, beside.at[step - 1], shifted.at[(n + 2) % 4])
                     advance_row(i + n, k, old, new, shifted.at[n], *coefs)
             if step == 2:
-                send_rows([i, i + 1], new, result, sem)
+                send_rows([i + n for n in range(4)], new, result, sem)
             return 0
 
-        lax.fori_loop(0, (ROWS - 2 - 2 * step) // 2, body, 0)
+        lax.fori_loop(0, count // 4, body, 0)
+        for n in range(count % 4):
+            i = low + count - count % 4 + n
+            for k in range(BANDS):
+                advance_row(i, k, old, new, shifted.at[n], *coefs)
+            send_rows([i], new, result, sem)
     sent = y.at[:, pl.ds(2 * GHOST, ROWS - 2 * GHOST), :, pl.ds(PAD, LEV), :]
     pltpu.make_async_copy(sent, sent, sem).wait()
 
@@ -507,7 +616,7 @@
 
 
 def rim_kernel(
-    got_first, got_second,
+    got_second, got_first,
     x_in, y_in, cc_in, ce_in, cw_in, cr_in, ct_in, ck_in, up_in, vp_in, dp_in, pe, result_in,
     x, y, cc, ce, cw, cr, ct, ck, up, vp, dp, result,
     shifted, e0, e1, eflow, ecoef, eck, edge_speed, beside, corners, sem,
@@ -522,20 +631,19 @@
         def plane(i):
             return GHOST + ROWS + i if north else GHOST - 1 - i
 
-        places = [(x.at[t], plane(i), PAD) for t in range(2) for i in range(3)]
-        places += [(vp, plane(j - 1 if north else j), 0) for j in range(3)]
-        places += [(up, plane(i), 0) for i in range(2)]
+        places = [(x.at[t], plane(i), PAD) for t in range(2) for i in range(2)]
+        places += [(vp, plane(j - 1 if north else j), 0) for j in range(2)]
+        places += [(up, plane(0), 0)] + [(y.at[t], plane(1), PAD) for t in range(2)]
         for n, (ref, i, offset) in enumerate(places):
-            if north and n == 6:
+            if north and n == 4:
                 continue
             for k in range(BANDS):
                 at = pl.ds(offset + 8 * k, 8)
                 tiles = [got[pl.ds((2 * n + half) * LEV + 8 * k, 8), :] for half in range(2)]
-                if north and 6 <= n < 9:
+                if north and n == 5:
                     tiles = [jnp.where(mirrored, -tile, tile) for tile in tiles]
-                if north and n >= 9:
-                    g = n - 9
-                    beyond = turned(corner[pl.ds(8 * k, 8), :], -8 * (2 * 4 + 2 + g) - 3)
+                if north and n == 6:
+                    beyond = turned(corner[pl.ds(8 * k, 8), :], -8 * (2 * 4 + 2) - 3)
                     moved = [turned(tile, -1) for tile in tiles]
                     east = [
                         jnp.where(lane == 127, moved[1], moved[0]),
@@ -598,10 +706,10 @@
 
     south, north = GHOST, GHOST + ROWS
 
-    for i in [south - 3 + j for j in range(3)] + [north - 1 + j for j in range(3)]:
+    for i in (south - 2, south - 1, north - 1, north):
         make_faces(i, vp, dp, cr, ct)
-    for j in range(3):
-        a, b = south - 2 + j, north - 1 + j
+    for j in range(2):
+        a, b = south - 1 + j, north - 1 + j
         for i in (a, b):
             make_column(i, dp, ck)
         make_cells([(a, 0, a), (b, 0, b - north + 13)], up, dp, edge_speed, *coefs)
@@ -609,8 +717,8 @@
     for step in range(3):
         old, new = (x, y) if step != 1 else (y, x)
         rows = []
-        for j in range(3):
-            a, b = south - 2 + step + j, north - 1 - step + j
+        for j in range(1 if step == 0 else 0, 3):
+            a, b = south - 2 + step + j, north + 1 - step - j
             rows += [(a, 0, a), (b, 0, b - north + 13)]
 
         def shift(n, rows=rows, old=old, step=step):
@@ -619,8 +727,8 @@
 
         shift(0)
         shift(1)
-        for n in range(6):
-            if n < 4:
+        for n in range(len(rows)):
+            if n + 2 < len(rows):
                 shift(n + 2)
             for k in range(BANDS):
                 advance_row(rows[n][0], k, old, new, shifted.at[n], *coefs)
@@ -653,6 +761,7 @@
 COLUMN = (PLANES, 2, DEEP, 128)
 DEPTH = (3, DROW + ROWS + 8, 128)
 SHIFTED = (2, 4, LEV, 128)
+AHEAD = (ROWS, *SHIFTED)
 EDGES = (4, 2, 2, LEV, 128)
 
 
@@ -683,48 +792,40 @@
 
 def local(tracers, u_east, v_north, bottom):
     lon_size, lat_size = lax.axis_size("lon"), lax.axis_size("lat")
-    inputs = (*far(tracers, u_east, v_north), bottom)
-    x, up, vp, dp, strip = call(
+    inputs = far(tracers, u_east, v_north, bottom)
+    x, up, vp, dp, strip, to_west, to_east = call(
         load_kernel,
         inputs,
-        [vmem(STATE), vmem(COEF), vmem(COEF), vmem(DEPTH), shape(STRIP, 128)],
-        in_specs=[IN_HBM] * 3 + [IN_VMEM],
-        out_specs=[IN_VMEM] * 5,
-        scratch_shapes=[pltpu.SemaphoreType.DMA((3,))],
+        [vmem(d) for d in [STATE, COEF, COEF, DEPTH, (STRIP, 128)]] + [shape(SENT, 128)] * 2,
+        in_specs=[IN_HBM] * 4,
+        out_specs=[IN_VMEM] * 7,
+        scratch_shapes=[pltpu.VMEM((ROWS, COLS), jnp.int32), pltpu.SemaphoreType.DMA((4,))],
         name="load",
     )
     eastward = [(i, (i + 1) % lon_size) for i in range(lon_size)]
-    from_west = lax.ppermute(strip, "lon", eastward)
-    from_east = lax.ppermute(strip, "lon", [(b, a) for a, b in eastward])
-    first, second = call(
-        rows_kernel,
+    from_west = lax.ppermute(to_east, "lon", eastward)
+    from_east = lax.ppermute(to_west, "lon", [(b, a) for a, b in eastward])
+    cc, ce, cw, cr, ct, ck, ahead, first, second = call(
+        early_kernel,
         near(x, up, vp, dp),
-        [vmem((PACKED, 128))] * 2,
+        [vmem(COEF)] * 5 + [vmem(COLUMN), vmem(AHEAD), vmem((PACKED, 128)), vmem((PACKED, 128))],
         in_specs=[IN_VMEM] * 4,
-        out_specs=[IN_VMEM] * 2,
+        out_specs=[IN_VMEM] * 9,
         scratch_shapes=[pltpu.SemaphoreType.DMA((2,))],
-        name="rows",
-        cost_estimate=cost(1_000_000, 4_000_000),
+        name="early",
+        cost_estimate=cost(12_000_000, 14_000_000),
     )
-    cr, ct, ck = call(
-        faces_kernel,
-        near(vp, dp),
-        [vmem(COEF), vmem(COEF), vmem(COLUMN)],
-        in_specs=[IN_VMEM] * 2,
-        out_specs=[IN_VMEM] * 3,
-        name="faces",
-        cost_estimate=cost(6_000_000, 8_000_000),
-    )
-    pe, dp, first, second = call(
+    dp, first, second, cc, ce, cw, pe, y, e0, ecoef, eck, patch, beside = call(
         corner_kernel,
-        (from_east, from_west, strip, *near(dp, first, second)),
-        [vmem(EDGES), vmem(DEPTH), vmem((PACKED, 128)), vmem((PACKED, 128))],
-        {3: 1, 4: 2, 5: 3},
-        in_specs=[IN_VMEM] * 6,
-        out_specs=[IN_VMEM] * 4,
+        (from_east, from_west, *near(strip, x, ahead, cr, ct, ck, dp, first, second, cc, ce, cw)),
+        [vmem(d) for d in [DEPTH, (PACKED, 128), (PACKED, 128)] + [COEF] * 3 + [EDGES, STATE]]
+        + [*edge_scratch(2)[1:4], vmem((2, 2, LEV, 128)), vmem((2, 2, LEV, 128))],
+        {8: 0, 9: 1, 10: 2, 11: 3, 12: 4, 13: 5},
+        in_specs=[IN_VMEM] * 14,
+        out_specs=[IN_VMEM] * 13,
+        scratch_shapes=[vmem((2, LEV, 128))],
         name="corner",
     )
-    got_first = lax.ppermute(first, "lat", [(lat, lat ^ 1) for lat in range(lat_size)])
     pairs = []
     for lon in range(lon_size):
         pairs.append((lon * lat_size, (lon ^ 1) * lat_size))
@@ -732,16 +833,19 @@
             pairs.append((lon * lat_size + lat, lon * lat_size + (lat + 1 if lat % 2 else lat - 1)))
         pairs.append((lon * lat_size + lat_size - 1, (lon_size - 1 - lon) * lat_size + lat_size - 1))
     got_second = lax.ppermute(second, ("lon", "lat"), pairs)
-
-    x, y, cc, ce, cw, result = call(
+    got_first = lax.ppermute(first, "lat", [(lat, lat ^ 1) for lat in range(lat_size)])
+
+    x, y, cc, ce, cw, result, _ = call(
         inner_kernel,
-        near(x, up, dp, cr, ct, ck, pe),
-        [vmem(STATE), vmem(STATE)] + [vmem(COEF)] * 3 + [shape(*tracers.shape)],
-        {0: 0},
-        limit=16,
-        in_specs=[IN_VMEM] * 7,
-        out_specs=[IN_VMEM] * 5 + [IN_HBM],
-        scratch_shapes=[vmem((2, *SHIFTED)), *edge_scratch(2), pltpu.SemaphoreType.DMA(())],
+        near(x, y, cc, ce, cw, cr, ct, ck, e0, ecoef, eck, patch, ahead, beside),
+        [vmem(STATE), vmem(STATE)] + [vmem(COEF)] * 3 + [shape(*tracers.shape), edge_scratch(2)[0]],
+        {0: 0, 1: 1, 2: 2, 3: 3, 4: 4, 8: 6},
+        limit=12,
+        in_specs=[IN_VMEM] * 14,
+        out_specs=[IN_VMEM] * 5 + [IN_HBM, IN_VMEM],
+        scratch_shapes=[
+            vmem((4, *SHIFTED)), edge_scratch(2)[0], vmem((2, 2, 2, LEV, 128)), pltpu.SemaphoreType.DMA(()),
+        ],
         name="inner",
         cost_estimate=cost(60_000_000, 20_000_000),
     )
@@ -750,7 +854,7 @@
     edge_lists = edge_scratch(1)
     return call(
         rim_kernel,
-        (got_first, got_second, *near(*held, pe), *far(result)),
+        (got_second, got_first, *near(*held, pe), *far(result)),
         [vmem(s) for s in sizes] + [shape(*tracers.shape)],
         {2 + n: n for n in range(11)} | {14: 11},
         limit=16,

time: 39.8 us -> 35.4 us (0.89)
  the two profiles are of different devices: /device:TPU:7 before, /device:TPU:68 now
where the time goes in v1:
time: 35.4 us; the launch traced here: 35.1 us
  Pallas kernels  25.6 us (72%)
  starting transfers between devices  8.08 us (23%)
  waiting for transfers between devices  1.38 us (4%)
    pallas_call x5, Pallas kernels, call(): pl.pallas_call(kernel, out_shape=outs, input_output_aliases=aliases or {}...  25.6 us
    ppermute x1, starting transfers between devices, local(): lax.ppermute(first, 'lat', [(lat, lat ^ 1) for lat in range(lat_size)])  4.74 us
    ppermute x1, starting transfers between devices, local(): from_east = lax.ppermute(to_west, 'lon', [(b, a) for a, b in eastward])  3.16 us
    ppermute x1, waiting for transfers between devices, local(): from_west = lax.ppermute(to_east, 'lon', eastward)  1.37 us
  transfers between devices with their start and end apart: 4, of which 1 were waited for; matrix products, arithmetic and copies ran while one was open for 0% of the time, Pallas kernels for 45%

profile of v1, /device:TPU:68, one launch (start us, length us, event | category | flops | bytes accessed | tf_op | source)
XLA Modules:
  0.0 35.1 jit_solution(11632486501785253944)
XLA Ops:
  0.0 4.9 %load.1 = (f32[2,38,2,64,128]{4,3,2,1,0:T(8,128)S(1)}, f32[38,2,48,128]{3,2,1,0:T(8,128)S(1)}, f32[38,2,48,128]{3,2,1,0:T(8,128)S(1)}, f32[3,48,128]{2,1,0:T(8,1...) custom-call(f32[2,48,32,256]{3,2,1,0:T(8,128)} %tr.1, f32[48,32,256]{2,1,0:T(8,128)} %u.1, ...), custom_call_target="tpu_custom_call" | custom-call | tf_op jit(solution)/shard_map/load/pallas_call | solution.py:780
  4.9 3.2 %collective-permute-start = (f32[224,128]{1,0:T(8,128)S(1)}, f32[224,128]{1,0:T(8,128)S(1)}, u32[]{:S(2)}, u32[]{:S(2)}) collective-permute-start(f32[224,128]{1,0:T(8,128)S(1)} %get-tuple-element.41), channel_id=1, source_target_pairs={{8,0},{16,8},{24,16},{32,24},{40,32},{48,40},{56,48},{64,56},{72,6... | collective-permute-start | bytes 344072 | tf_op jit(solution)/shard_map/ppermute | solution.py:807
  8.1 0.0 collective-permute-start.1
  8.1 4.9 %early.1 = (f32[38,2,48,128]{3,2,1,0:T(8,128)S(1)}, f32[38,2,48,128]{3,2,1,0:T(8,128)S(1)}, f32[38,2,48,128]{3,2,1,0:T(8,128)S(1)}, f32[38,2,48,128]{3,2,1,0:T(8...) custom-call(f32[2,38,2,64,128]{4,3,2,1,0:T(8,128)S(1)} %get-tuple-el, ...), custom_call_target="tpu_custom_call" | custom-call | flops 12000000 | bytes 14000000 | tf_op jit(solution)/shard_map/early/pallas_call | solution.py:780
  13.0 0.0 collective-permute-done.from_east
  13.0 1.4 %collective-permute-done.1.from_west = f32[224,128]{1,0:T(8,128)S(1)} collective-permute-done((f32[224,128]{1,0:T(8,128)S(1)}, f32[224,128]{1,0:T(8,128)S(1)}, u32[]{:S(2)}, u32[]{:S(2)}) %collective-permute-start.1) | collective-permute-done | bytes 114720 | tf_op jit(solution)/shard_map/ppermute | solution.py:806
  14.4 1.2 %corner.1 = (f32[3,48,128]{2,1,0:T(8,128)S(1)}, f32[944,128]{1,0:T(8,128)S(1)}, f32[944,128]{1,0:T(8,128)S(1)}, f32[38,2,48,128]{3,2,1,0:T(8,128)S(1)}, f32[38,2...) custom-call(f32[224,128]{1,0:T(8,128)S(1)} %collective-permute-done., ...), custom_call_target="tpu_custom_call", output_to_operand_aliasing={{0}: (8, {}), {1}: (9, {}), {2}: (10, {}), {3}: (11, {}), {... | custom-call | tf_op jit(solution)/shard_map/corner/pallas_call | solution.py:780
  15.6 0.2 collective-permute-start.2
  15.8 4.7 %collective-permute-start.3 = (f32[944,128]{1,0:T(8,128)S(1)}, f32[944,128]{1,0:T(8,128)S(1)}, u32[]{:S(2)}, u32[]{:S(2)}) collective-permute-start(f32[944,128]{1,0:T(8,128)S(1)} %get-tuple-element.58), channel_id=1, source_target_pairs={{0,1},{1,0},{2,3},{3,2},{4,5},{5,4},{6,7},{7,6},{8,9},{9,8},{10,11... | collective-permute-start | bytes 1449992 | tf_op jit(solution)/shard_map/ppermute | solution.py:836
  20.5 10.8 %inner.1 = (f32[2,38,2,64,128]{4,3,2,1,0:T(8,128)S(1)}, f32[2,38,2,64,128]{4,3,2,1,0:T(8,128)S(1)}, f32[38,2,48,128]{3,2,1,0:T(8,128)S(1)}, f32[38,2,48,128]{3,2...) custom-call(f32[2,38,2,64,128]{4,3,2,1,0:T(8,128)S(1)} %get-tuple-el, ...), custom_call_target="tpu_custom_call", output_to_operand_aliasing={{0}: (0, {}), {1}: (1, {}), {2}: (2, {}), {3}: (3, {}), {4}... | custom-call | flops 60000000 | bytes 20000000 | tf_op jit(solution)/shard_map/inner/pallas_call | solution.py:780
  31.3 0.0 collective-permute-done.2.got_second
  31.3 0.0 collective-permute-done.3.got_first
  31.3 3.8 %rim.1 = (f32[2,38,2,64,128]{4,3,2,1,0:T(8,128)S(1)}, f32[2,38,2,64,128]{4,3,2,1,0:T(8,128)S(1)}, f32[38,2,48,128]{3,2,1,0:T(8,128)S(1)}, f32[38,2,48,128]{3,2,1...) custom-call(f32[944,128]{1,0:T(8,128)S(1)} %collective-permute-done., ...), custom_call_target="tpu_custom_call", output_to_operand_aliasing={{0}: (2, {}), {1}: (3, {}), {2}: (4, {}), {3}: (5, {}), {4}... | custom-call | tf_op jit(solution)/shard_map/rim/pallas_call | solution.py:780
Async XLA Ops:
  4.9 8.1 %collective-permute-start = (f32[224,128]{1,0:T(8,128)S(1)}, f32[224,128]{1,0:T(8,128)S(1)}, u32[]{:S(2)}, u32[]{:S(2)}) collective-permute-start(f32[224,128]{1,0:T(8,128)S(1)} %get-tuple-element.41), channel_id=1, source_target_pairs={{8,0},{16,8},{24,16},{32,24},{40,32},{48,40},{56,48},{64,56},{72,6... | collective-permute-start | bytes 344072 | tf_op jit(solution)/shard_map/ppermute | solution.py:807
  8.1 6.3 %collective-permute-start.1 = (f32[224,128]{1,0:T(8,128)S(1)}, f32[224,128]{1,0:T(8,128)S(1)}, u32[]{:S(2)}, u32[]{:S(2)}) collective-permute-start(f32[224,128]{1,0:T(8,128)S(1)} %get-tuple-element.42), channel_id=1, source_target_pairs={{0,8},{8,16},{16,24},{24,32},{32,40},{40,48},{48,56},{56,64},{64,7... | collective-permute-start | bytes 344072 | tf_op jit(solution)/shard_map/ppermute | solution.py:806
  15.6 15.7 %collective-permute-start.2 = (f32[944,128]{1,0:T(8,128)S(1)}, f32[944,128]{1,0:T(8,128)S(1)}, u32[]{:S(2)}, u32[]{:S(2)}) collective-permute-start(f32[944,128]{1,0:T(8,128)S(1)} %get-tuple-element.57), channel_id=1, source_target_pairs={{0,8},{1,2},{2,1},{3,4},{4,3},{5,6},{6,5},{7,127},{8,0},{9,10},{10... | collective-permute-start | bytes 1449992 | tf_op jit(solution)/shard_map/ppermute | solution.py:835
  15.8 15.5 %collective-permute-start.3 = (f32[944,128]{1,0:T(8,128)S(1)}, f32[944,128]{1,0:T(8,128)S(1)}, u32[]{:S(2)}, u32[]{:S(2)}) collective-permute-start(f32[944,128]{1,0:T(8,128)S(1)} %get-tuple-element.58), channel_id=1, source_target_pairs={{0,1},{1,0},{2,3},{3,2},{4,5},{5,4},{6,7},{7,6},{8,9},{9,8},{10,11... | collective-permute-start | bytes 1449992 | tf_op jit(solution)/shard_map/ppermute | solution.py:836

commit v2 on v1

--- a/solution.py
+++ b/solution.py
@@ -15,6 +15,7 @@
 PLANES = ROWS + 2 * GHOST
 PAD = 8
 DEEP = 64
+NEAR = (GHOST + 1, GHOST + ROWS - 2)
 DROW = 8
 COPIED = 7
 ITEMS = COPIED + 2
@@ -42,6 +43,10 @@
     return jnp.take_along_axis(x, index, axis=1)
 
 
+def lane_tile(n):
+    return pl.ds(128 * n, 128)
+
+
 def is_top():
     return lax.axis_index("lat") == lax.axis_size("lat") - 1
 
@@ -70,12 +75,12 @@
         def face(j):
             return jnp.where(north, ROWS - 1 - j, 0) + GHOST
 
-        items = [(x.at[t], row(i), PAD) for t in range(2) for i in range(2)]
-        items += [(vp, face(0), 0), (vp, face(1), 0), (up, row(0), 0)]
-        for n, (ref, i, offset) in enumerate(items):
+        items = [(x.at[t], row(i)) for t in range(2) for i in range(2)]
+        items += [(vp, face(0)), (vp, face(1)), (up, row(0))]
+        for n, (ref, i) in enumerate(items):
             for half in range(2):
                 pltpu.make_async_copy(
-                    ref.at[i, half, pl.ds(offset, LEV), :],
+                    ref.at[i, half, pl.ds(PAD, LEV), :] if n < 4 else ref.at[i, :, lane_tile(half)],
                     out.at[pl.ds((2 * n + half) * LEV, LEV), :],
                     sem,
                 ).start()
@@ -119,9 +124,7 @@
     wet_copy.start()
     for source, into, sem in ((u, up, sems.at[1]), (v, vp, sems.at[2])):
         for r in range(ROWS):
-            for half in range(2):
-                columns = pl.ds(128 * half, 128)
-                pltpu.make_async_copy(source.at[:, r, columns], into.at[r + GHOST, half], sem).start()
+            pltpu.make_async_copy(source.at[:, r, :], into.at[r + GHOST], sem).start()
 
     def start_tracers(r):
         for half in range(2):
@@ -190,10 +193,9 @@
 
             @pl.when(is_top())
             def _():
-                for half in range(2):
-                    vp[GHOST + ROWS - 1, half] = jnp.zeros((LEV, 128), F32)
-
-        pack(n + 1, lambda i, k, ref=ref: [ref[i, half, pl.ds(8 * k, 8), :] for half in range(2)], n == 1)
+                vp[GHOST + ROWS - 1] = jnp.zeros((LEV, COLS), F32)
+
+        pack(n + 1, lambda i, k, ref=ref: [ref[i, pl.ds(8 * k, 8), lane_tile(half)] for half in range(2)], n == 1)
     whole = x.at[:, own, :, pl.ds(PAD, LEV), :]
     pltpu.make_async_copy(whole, whole, sems.at[0]).wait()
     for t in range(2):
@@ -228,7 +230,7 @@
         least = jnp.minimum(here[n], north[n])
         for k in range(BANDS):
             at = pl.ds(8 * k, 8)
-            speed = vp[i, n, at, :]
+            speed = vp[i, at, lane_tile(n)]
             opened = level_of(k) < least
             cr[i, n, at, :] = forth(speed, opened)
             ct[i, n, at, :] = back(speed, opened)
@@ -252,7 +254,7 @@
     for k in range(BANDS):
         at = pl.ds(8 * k, 8)
         for (i, part, slot), least in zip(rows, leasts):
-            speeds = [jnp.where(level_of(k) < least[n], up[i, n, at, :], SHUT) for n in range(2)]
+            speeds = [jnp.where(level_of(k) < least[n], up[i, at, lane_tile(n)], SHUT) for n in range(2)]
             a, b = [turned(speed, 1) for speed in speeds]
             outer = a if edge_speed is None else turned(edge_speed[part, at, :], -8 * slot - 2)
             wests = [jnp.where(lane == 0, outer, a), jnp.where(lane == 0, a, b)]
@@ -295,6 +297,8 @@
     lane = lanes()
     depth_e = [turned(d, -1) for d in depths]
     depth_n = next_slot(depths, lane)
+    if parts == 2:
+        depth_n[1] = jnp.where(lane >= 120, 0.0, depth_n[1])
     every = range(parts)
     for k in range(BANDS):
         at = pl.ds(8 * k, 8)
@@ -371,6 +375,7 @@
 def early_kernel(x, up, vp, dp, cc, ce, cw, cr, ct, ck, beside, first, second, sems):
     end = row_copies(x, up, vp, dp, first, second, sems)
     lane = lanes()
+    ct[GHOST - 1] = jnp.zeros((2, LEV, 128), F32)
 
     def one(j, _):
         for n in range(2):
@@ -379,24 +384,25 @@
             make_faces(i, vp, dp, cr, ct)
             make_column(i, dp, ck)
             make_cells([(i, 0, 0)], up, dp, None, cc, ce, cw, cr, ct, ck)
-            for k in range(BANDS):
-                at = pl.ds(8 * k, 8)
-                here = pl.ds(PAD + 8 * k, 8)
-                for t in range(2):
-                    left, right = x[t, i, 0, here, :], x[t, i, 1, here, :]
-                    right_e, left_w = turned(right, -1), turned(left, 1)
-                    beside[r, t, 0, at, :] = jnp.where(lane == 127, right_e, turned(left, -1))
-                    beside[r, t, 1, at, :] = right_e
-                    beside[r, t, 2, at, :] = left_w
-                    beside[r, t, 3, at, :] = jnp.where(lane == 0, left_w, turned(right, 1))
         return 0
 
     lax.fori_loop(0, ROWS // 2, one, 0)
+    for n, i in enumerate(NEAR):
+        for k in range(BANDS):
+            at = pl.ds(8 * k, 8)
+            here = pl.ds(PAD + 8 * k, 8)
+            for t in range(2):
+                left, right = x[t, i, 0, here, :], x[t, i, 1, here, :]
+                right_e, left_w = turned(right, -1), turned(left, 1)
+                beside[n, t, 0, at, :] = jnp.where(lane == 127, right_e, turned(left, -1))
+                beside[n, t, 1, at, :] = right_e
+                beside[n, t, 2, at, :] = left_w
+                beside[n, t, 3, at, :] = jnp.where(lane == 0, left_w, turned(right, 1))
     end()
 
 
 def corner_kernel(
-    from_east, from_west, strip, x, ahead, cr, ct, ck, dp_in, first_in, second_in, cc_in, ce_in, cw_in,
+    from_west, from_east, strip, x, ahead, cr, ct, ck, dp_in, first_in, second_in, cc_in, ce_in, cw_in,
     dp, first, second, cc, ce, cw, pe, y, e0, ecoef, eck, patch, beside, edge_speed,
 ):
     lane = lanes()
@@ -457,12 +463,11 @@
             patch[0, p, at, :] = jnp.where(last, ecoef[1, p, 0, at, :], ecoef[0, p, 0, at, :])
             patch[1, p, at, :] = jnp.where(last, ecoef[1, p, 1, at, :], ecoef[0, p, 2, at, :])
     edge_beside(2, e0, beside)
-    near_south, near_north = GHOST + 1, GHOST + ROWS - 2
     for k in range(BANDS):
-        for row in ((near_south, 0, 1), (near_north, 1, 14)):
-            first_row(row, k, x, y, ahead, beside, patch, cc, ce, cw, cr, ct, ck)
+        for n, row in enumerate(((NEAR[0], 0, 1), (NEAR[1], 1, 14))):
+            first_row(row, k, x, y, ahead.at[n], beside, patch, cc, ce, cw, cr, ct, ck)
     for out, north in ((first, is_even()), (second, jnp.logical_not(is_even()))):
-        i = jnp.where(north, near_north, near_south)
+        i = jnp.where(north, NEAR[1], NEAR[0])
         for t in range(2):
             for half in range(2):
                 at = pl.ds((2 * (COPIED + t) + half) * LEV, LEV)
@@ -498,7 +503,7 @@
         shifted[t, 3, at, :] = jnp.where(lane == 0, left_w, right_w)
 
 
-def advance_row(i, k, old, new, shifted, cc, ce, cw, cr, ct, ck):
+def advance_row(i, k, old, put, shifted, cc, ce, cw, cr, ct, ck, without=None):
     at = pl.ds(8 * k, 8)
     here = pl.ds(PAD + 8 * k, 8)
     above = pl.ds(PAD + 8 * k - 1, 8)
@@ -510,22 +515,34 @@
         for t in range(2):
             total = c_c * old[t, i, n, here, :]
             total += c_e * shifted[t, n, at, :] + c_w * shifted[t, 2 + n, at, :]
-            total += c_n * old[t, i + 1, n, here, :] + c_s * old[t, i - 1, n, here, :]
+            if without != "north":
+                total += c_n * old[t, i + 1, n, here, :]
+            if without != "south":
+                total += c_s * old[t, i - 1, n, here, :]
             total += c_u * old[t, i, n, above, :] + c_d * old[t, i, n, below, :]
-            new[t, i, n, here, :] = total
-
-
-def send_rows(rows, new, result, sem):
-    for i in rows:
-        for half in range(2):
-            pltpu.make_async_copy(
-                new.at[:, i, half, pl.ds(PAD, LEV), :],
-                result.at[:, :, i - GHOST, pl.ds(128 * half, 128)],
-                sem,
-            ).start()
-
-
-def first_row(row, k, old, new, ahead, beside, patch, cc, ce, cw, cr, ct, ck):
+            put[t, n, pl.ds(put.shape[2] - LEV - PAD * (put.shape[2] > LEV) + 8 * k, 8), :] = total
+
+
+def send_row(row, r, result, sem):
+    for half in range(2):
+        pltpu.make_async_copy(
+            row.at[:, half], result.at[:, :, r, pl.ds(128 * half, 128)], sem
+        ).start()
+
+
+def patch_row(row, k, patch, cc, ce, cw):
+    i, part, slot = row
+    lane = lanes()
+    at = pl.ds(8 * k, 8)
+    centre = turned(patch[0, part, at, :], -8 * slot - 3)
+    sides = turned(patch[1, part, at, :], -8 * slot - 3)
+    cc[i, 0, at, :] = jnp.where(lane == 0, centre, cc[i, 0, at, :])
+    cc[i, 1, at, :] = jnp.where(lane == 127, centre, cc[i, 1, at, :])
+    cw[i, 0, at, :] = jnp.where(lane == 0, sides, cw[i, 0, at, :])
+    ce[i, 1, at, :] = jnp.where(lane == 127, sides, ce[i, 1, at, :])
+
+
+def first_row(row, k, old, new, shifted, beside, patch, cc, ce, cw, cr, ct, ck):
     i, part, slot = row
     lane = lanes()
     at = pl.ds(8 * k, 8)
@@ -535,7 +552,8 @@
     edge = [lane == 0, lane == 127]
     centre = turned(patch[0, part, at, :], -8 * slot - 3)
     sides = turned(patch[1, part, at, :], -8 * slot - 3)
-    outer = [turned(beside[t, part, at, :], -8 * slot - 4) for t in range(2)]
+    if beside is not None:
+        outer = [turned(beside[t, part, at, :], -8 * slot - 4) for t in range(2)]
     for n in range(2):
         c_c = jnp.where(edge[n], centre, cc[i, n, at, :])
         cc[i, n, at, :] = c_c
@@ -549,8 +567,10 @@
         c_n, c_s = ct[i, n, at, :], cr[i - 1, n, at, :]
         c_d, c_u = ck[i, n, here, :], ck[i, n, above, :]
         for t in range(2):
-            east, west = ahead[i - GHOST, t, n, at, :], ahead[i - GHOST, t, 2 + n, at, :]
-            if n == 0:
+            east, west = shifted[t, n, at, :], shifted[t, 2 + n, at, :]
+            if beside is None:
+                pass
+            elif n == 0:
                 west = jnp.where(edge[0], outer[t], west)
             else:
                 east = jnp.where(edge[1], outer[t], east)
@@ -561,52 +581,80 @@
 
 
 def inner_kernel(
-    x_in, y_in, cc_in, ce_in, cw_in, cr, ct, ck, e0_in, ecoef, eck, patch, ahead, beside_in,
-    x, y, cc, ce, cw, result, e0, shifted, e1, beside, sem,
+    x_in, y_in, cc_in, ce_in, cw_in, cr, ct, ck, e0_in, ecoef, eck, patch, beside_in,
+    x, y, cc, ce, cw, result, e0, partial, shifted, e1, beside, sem,
 ):
     coefs = (cc, ce, cw, cr, ct, ck)
+
+    def part_of_rows(step, old, beyond):
+        for n, r in enumerate((step, ROWS - 1 - step)):
+            row = (r + GHOST, r // 16, r % 16)
+            for k in range(BANDS):
+                shift_row(row, k, old, beyond, shifted.at[n])
+        for n, r in enumerate((step, ROWS - 1 - step)):
+            for k in range(BANDS):
+                if step == 0:
+                    patch_row((r + GHOST, r // 16, r % 16), k, patch, cc, ce, cw)
+                put, without = partial.at[step, n], "north" if n else "south"
+                advance_row(r + GHOST, k, old, put, shifted.at[n], *coefs, without)
+
+    part_of_rows(0, x, beside_in)
 
     def placed(i):
         i = jnp.minimum(i, GHOST + ROWS - 1)
         return i, (i - GHOST) // 16, (i - GHOST) % 16
 
+    for n in range(2):
+        for k in range(BANDS):
+            shift_row(placed(GHOST + 2 + n), k, x, beside_in, shifted.at[n])
+
     def first(j, _):
-        for n in range(2):
+        for n in range(RING):
+            i = GHOST + 2 + RING * j + n
             for k in range(BANDS):
-                first_row(placed(GHOST + 2 + 2 * j + n), k, x, y, ahead, beside_in, patch, *coefs)
+                shift_row(placed(i + 2), k, x, beside_in, shifted.at[(n + 2) % RING])
+                first_row(placed(i), k, x, y, shifted.at[n], None, patch, *coefs)
         return 0
 
-    lax.fori_loop(0, ROWS // 2 - 2, first, 0)
+    lax.fori_loop(0, (ROWS - 4) // RING, first, 0)
     clear_levels(e1)
     edge_step(2, e0, e1, ecoef, eck)
     edge_beside(2, e1, beside.at[0])
     edge_step(2, e1, e0, ecoef, eck)
     edge_beside(2, e0, beside.at[1])
-
-    for step in range(1, 3):
-        old, new = (x, y) if step != 1 else (y, x)
-        low = GHOST + 1 + step
-        count = ROWS - 2 - 2 * step
-        for n in range(2):
+    part_of_rows(1, y, beside.at[0])
+
+    for n in range(2):
+        for k in range(BANDS):
+            shift_row(placed(GHOST + 2 + n), k, y, beside.at[0], shifted.at[n])
+
+    def second(j, _):
+        for n in range(RING):
+            i = GHOST + 2 + RING * j + n
             for k in range(BANDS):
-                shift_row(placed(low + n), k, old, beside.at[step - 1], shifted.at[n])
-
-        def body(j, _, low=low, old=old, new=new, step=step):
-            i = low + 4 * j
-            for n in range(4):
-                for k in range(BANDS):
-                    shift_row(placed(i + n + 2), k, old, beside.at[step - 1], shifted.at[(n + 2) % 4])
-                    advance_row(i + n, k, old, new, shifted.at[n], *coefs)
-            if step == 2:
-                send_rows([i + n for n in range(4)], new, result, sem)
-            return 0
-
-        lax.fori_loop(0, count // 4, body, 0)
-        for n in range(count % 4):
-            i = low + count - count % 4 + n
+                shift_row(placed(i + 2), k, y, beside.at[0], shifted.at[(n + 2) % RING])
+                advance_row(i, k, y, x.at[:, i], shifted.at[n], *coefs)
+        return 0
+
+    lax.fori_loop(0, (ROWS - 4) // RING, second, 0)
+
+    part_of_rows(2, x, beside.at[1])
+    for n in range(2):
+        for k in range(BANDS):
+            shift_row(placed(2 * GHOST + n), k, x, beside.at[1], shifted.at[n])
+
+    def third(j, _):
+        for n in range(GROUP):
+            i = 2 * GHOST + GROUP * j + n
             for k in range(BANDS):
-                advance_row(i, k, old, new, shifted.at[n], *coefs)
-            send_rows([i], new, result, sem)
+                shift_row(placed(i + 2), k, x, beside.at[1], shifted.at[(n + 2) % GROUP])
+                advance_row(i, k, x, y.at[:, i], shifted.at[n], *coefs)
+        for n in range(GROUP):
+            i = 2 * GHOST + GROUP * j + n
+            send_row(y.at[:, i, :, pl.ds(PAD, LEV), :], i - GHOST, result, sem)
+        return 0
+
+    lax.fori_loop(0, (ROWS - 2 * GHOST) // GROUP, third, 0)
     sent = y.at[:, pl.ds(2 * GHOST, ROWS - 2 * GHOST), :, pl.ds(PAD, LEV), :]
     pltpu.make_async_copy(sent, sent, sem).wait()
 
@@ -617,9 +665,9 @@
 
 def rim_kernel(
     got_second, got_first,
-    x_in, y_in, cc_in, ce_in, cw_in, cr_in, ct_in, ck_in, up_in, vp_in, dp_in, pe, result_in,
+    x_in, y_in, cc_in, ce_in, cw_in, cr_in, ct_in, ck_in, up_in, vp_in, dp_in, pe, partial, result_in,
     x, y, cc, ce, cw, cr, ct, ck, up, vp, dp, result,
-    shifted, e0, e1, eflow, ecoef, eck, edge_speed, beside, corners, sem,
+    shifted, e0, e1, eflow, ecoef, eck, edge_speed, beside, corners, sem, *outs,
 ):
     lane = lanes()
     coefs = (cc, ce, cw, cr, ct, ck)
@@ -651,7 +699,10 @@
                     ]
                     tiles = [jnp.where(mirrored, -b, a) for a, b in zip(tiles, east)]
                 for half in range(2):
-                    ref[i, half, at, :] = tiles[half]
+                    if 4 <= n < 7:
+                        ref[i, at, lane_tile(half)] = tiles[half]
+                    else:
+                        ref[i, half, at, :] = tiles[half]
         for i in range(3):
             at = pl.ds(plane(i) - GHOST + DROW, 1)
             rows = [got[pl.ds(DEPTHS + 2 * i + half, 1), :] for half in range(2)]
@@ -708,34 +759,58 @@
 
     for i in (south - 2, south - 1, north - 1, north):
         make_faces(i, vp, dp, cr, ct)
-    for j in range(2):
-        a, b = south - 1 + j, north - 1 + j
-        for i in (a, b):
-            make_column(i, dp, ck)
-        make_cells([(a, 0, a), (b, 0, b - north + 13)], up, dp, edge_speed, *coefs)
+    for i in (south - 1, north):
+        make_column(i, dp, ck)
+    make_cells([(south - 1, 0, south - 1), (north, 0, 13)], up, dp, edge_speed, *coefs)
+    for n in range(2):
+        for k in range(BANDS):
+            at = pl.ds(8 * k, 8)
+            cc[south, n, at, :] = cc[south, n, at, :] - ct[south - 1, n, at, :]
+            cc[north - 1, n, at, :] = cc[north - 1, n, at, :] - cr[north - 1, n, at, :]
+
+    def complete(i, old, put, share, from_south, step):
+        for n in range(2):
+            for k in range(BANDS):
+                at = pl.ds(8 * k, 8)
+                here = pl.ds(PAD + 8 * k, 8)
+                inward = cr[i - 1, n, at, :] if from_south else ct[i, n, at, :]
+                outward = ct[i - 1, n, at, :] if from_south else cr[i, n, at, :]
+                for t in range(2):
+                    beyond = old[t, i - 1 if from_south else i + 1, n, here, :]
+                    total = share[t, n, at, :] + inward * beyond
+                    if step == 0:
+                        total -= outward * old[t, i, n, here, :]
+                    put[t, n, pl.ds(put.shape[2] - LEV - PAD * (put.shape[2] > LEV) + 8 * k, 8), :] = total
 
     for step in range(3):
         old, new = (x, y) if step != 1 else (y, x)
-        rows = []
-        for j in range(1 if step == 0 else 0, 3):
-            a, b = south - 2 + step + j, north + 1 - step - j
-            rows += [(a, 0, a), (b, 0, b - north + 13)]
+        rows = [(south - 1, north), (south - 1, north, south, north - 1), (south, north - 1, south + 1, north - 2)][step]
 
         def shift(n, rows=rows, old=old, step=step):
+            i = rows[n]
+            row = (i, 0, i if i < 16 else i - north + 13)
             for k in range(BANDS):
-                shift_row(rows[n], k, old, beside.at[step], shifted.at[n])
+                shift_row(row, k, old, beside.at[step], shifted.at[n])
 
         shift(0)
         shift(1)
-        for n in range(len(rows)):
+        for n, i in enumerate((south + step, north - 1 - step)):
+            put = outs[n] if step == 2 else new.at[:, i]
+            complete(i, old, put, partial.at[step, n], n == 0, step)
+        if step == 2:
+            send_row(outs[0], 2, result, sem)
+            send_row(outs[1], ROWS - 3, result, sem)
+        for n, i in enumerate(rows):
             if n + 2 < len(rows):
                 shift(n + 2)
             for k in range(BANDS):
-                advance_row(rows[n][0], k, old, new, shifted.at[n], *coefs)
-    for start in (south, north - GHOST):
-        send_rows([start + n for n in range(3)], y, result, sem)
-    sent = y.at[:, pl.ds(0, 2 * GHOST), :, pl.ds(PAD, LEV), :]
-    pltpu.make_async_copy(sent, sent, sem).wait()
+                put = outs[2 + n] if step == 2 else new.at[:, i]
+                advance_row(i, k, old, put, shifted.at[n], *coefs)
+            if step == 2 and n:
+                send_row(outs[1 + n], rows[n - 1] - GHOST, result, sem)
+    send_row(outs[5], rows[3] - GHOST, result, sem)
+    for out in outs:
+        pltpu.make_async_copy(out, out, sem).wait()
 
 
 def shape(*dims):
@@ -758,10 +833,13 @@
 IN_HBM = pl.BlockSpec(memory_space=pltpu.HBM)
 STATE = (2, PLANES, 2, DEEP, 128)
 COEF = (PLANES, 2, LEV, 128)
+FLOW = (PLANES, LEV, COLS)
 COLUMN = (PLANES, 2, DEEP, 128)
 DEPTH = (3, DROW + ROWS + 8, 128)
 SHIFTED = (2, 4, LEV, 128)
-AHEAD = (ROWS, *SHIFTED)
+RING = 14
+GROUP = 13
+AHEAD = (2, *SHIFTED)
 EDGES = (4, 2, 2, LEV, 128)
 
 
@@ -796,7 +874,7 @@
     x, up, vp, dp, strip, to_west, to_east = call(
         load_kernel,
         inputs,
-        [vmem(d) for d in [STATE, COEF, COEF, DEPTH, (STRIP, 128)]] + [shape(SENT, 128)] * 2,
+        [vmem(d) for d in [STATE, FLOW, FLOW, DEPTH, (STRIP, 128)]] + [shape(SENT, 128)] * 2,
         in_specs=[IN_HBM] * 4,
         out_specs=[IN_VMEM] * 7,
         scratch_shapes=[pltpu.VMEM((ROWS, COLS), jnp.int32), pltpu.SemaphoreType.DMA((4,))],
@@ -817,7 +895,7 @@
     )
     dp, first, second, cc, ce, cw, pe, y, e0, ecoef, eck, patch, beside = call(
         corner_kernel,
-        (from_east, from_west, *near(strip, x, ahead, cr, ct, ck, dp, first, second, cc, ce, cw)),
+        (from_west, from_east, *near(strip, x, ahead, cr, ct, ck, dp, first, second, cc, ce, cw)),
         [vmem(d) for d in [DEPTH, (PACKED, 128), (PACKED, 128)] + [COEF] * 3 + [EDGES, STATE]]
         + [*edge_scratch(2)[1:4], vmem((2, 2, LEV, 128)), vmem((2, 2, LEV, 128))],
         {8: 0, 9: 1, 10: 2, 11: 3, 12: 4, 13: 5},
@@ -835,34 +913,34 @@
     got_second = lax.ppermute(second, ("lon", "lat"), pairs)
     got_first = lax.ppermute(first, "lat", [(lat, lat ^ 1) for lat in range(lat_size)])
 
-    x, y, cc, ce, cw, result, _ = call(
+    x, y, cc, ce, cw, result, _, partial = call(
         inner_kernel,
-        near(x, y, cc, ce, cw, cr, ct, ck, e0, ecoef, eck, patch, ahead, beside),
-        [vmem(STATE), vmem(STATE)] + [vmem(COEF)] * 3 + [shape(*tracers.shape), edge_scratch(2)[0]],
+        near(x, y, cc, ce, cw, cr, ct, ck, e0, ecoef, eck, patch, beside),
+        [vmem(STATE), vmem(STATE)] + [vmem(COEF)] * 3 + [shape(*tracers.shape), edge_scratch(2)[0], vmem((3, 2, 2, 2, LEV, 128))],
         {0: 0, 1: 1, 2: 2, 3: 3, 4: 4, 8: 6},
         limit=12,
-        in_specs=[IN_VMEM] * 14,
-        out_specs=[IN_VMEM] * 5 + [IN_HBM, IN_VMEM],
+        in_specs=[IN_VMEM] * 13,
+        out_specs=[IN_VMEM] * 5 + [IN_HBM, IN_VMEM, IN_VMEM],
         scratch_shapes=[
-            vmem((4, *SHIFTED)), edge_scratch(2)[0], vmem((2, 2, 2, LEV, 128)), pltpu.SemaphoreType.DMA(()),
+            vmem((RING, *SHIFTED)), edge_scratch(2)[0], vmem((2, 2, 2, LEV, 128)), pltpu.SemaphoreType.DMA(()),
         ],
         name="inner",
         cost_estimate=cost(60_000_000, 20_000_000),
     )
     held = [x, y, cc, ce, cw, cr, ct, ck, up, vp, dp]
-    sizes = [STATE, STATE] + [COEF] * 5 + [COLUMN, COEF, COEF, DEPTH]
+    sizes = [STATE, STATE] + [COEF] * 5 + [COLUMN, FLOW, FLOW, DEPTH]
     edge_lists = edge_scratch(1)
     return call(
         rim_kernel,
-        (got_second, got_first, *near(*held, pe), *far(result)),
+        (got_second, got_first, *near(*held, pe, partial), *far(result)),
         [vmem(s) for s in sizes] + [shape(*tracers.shape)],
-        {2 + n: n for n in range(11)} | {14: 11},
+        {2 + n: n for n in range(11)} | {15: 11},
         limit=16,
-        in_specs=[IN_VMEM] * 14 + [IN_HBM],
+        in_specs=[IN_VMEM] * 15 + [IN_HBM],
         out_specs=[IN_VMEM] * 11 + [IN_HBM],
         scratch_shapes=[
             vmem((6, *SHIFTED)), *edge_lists[:2], vmem((2, 2, 1, LEV, 128)), *edge_lists[2:],
-            vmem((2, LEV, 128)), pltpu.SemaphoreType.DMA(()),
+            vmem((2, LEV, 128)), pltpu.SemaphoreType.DMA(()), *[vmem((2, 2, LEV, 128))] * 6,
         ],
         name="rim",
     )[-1]

time: 35.4 us -> 34.2 us (0.966)
  the two profiles are of different devices: /device:TPU:68 before, /device:TPU:7 now
where the time goes in v2:
time: 34.2 us; the launch traced here: 33.9 us
  Pallas kernels  23.5 us (69%)
  starting transfers between devices  6.58 us (19%)
  waiting for transfers between devices  3.79 us (11%)
    pallas_call x5, Pallas kernels, call(): pl.pallas_call(kernel, out_shape=outs, input_output_aliases=aliases or {}...  23.5 us
    ppermute x1, starting transfers between devices, local(): got_second = lax.ppermute(second, ('lon', 'lat'), pairs)  4.38 us
    ppermute x1, starting transfers between devices, local(): from_west = lax.ppermute(to_east, 'lon', eastward)  2.19 us
    ppermute x1, waiting for transfers between devices, local(): lax.ppermute(first, 'lat', [(lat, lat ^ 1) for lat in range(lat_size)])  1.51 us
    ppermute x1, waiting for transfers between devices, local(): from_east = lax.ppermute(to_west, 'lon', [(b, a) for a, b in eastward])  1.39 us
    ppermute x1, waiting for transfers between devices, local(): got_second = lax.ppermute(second, ('lon', 'lat'), pairs)  0.89 us
  transfers between devices with their start and end apart: 4, of which 3 were waited for; matrix products, arithmetic and copies ran while one was open for 0% of the time, Pallas kernels for 42%

profile of v2, /device:TPU:7, one launch (start us, length us, event | category | flops | bytes accessed | tf_op | source)
XLA Modules:
  0.0 33.9 jit_solution(8871949025104850313)
XLA Ops:
  0.0 4.9 %load.1 = (f32[2,38,2,64,128]{4,3,2,1,0:T(8,128)S(1)}, f32[38,48,256]{2,1,0:T(8,128)S(1)}, f32[38,48,256]{2,1,0:T(8,128)S(1)}, f32[3,48,128]{2,1,0:T(8,128)S(1)}...) custom-call(f32[2,48,32,256]{3,2,1,0:T(8,128)} %tr.1, f32[48,32,256]{2,1,0:T(8,128)} %u.1, ...), custom_call_target="tpu_custom_call" | custom-call | tf_op jit(solution)/shard_map/load/pallas_call | solution.py:858
  4.9 2.2 %collective-permute-start = (f32[224,128]{1,0:T(8,128)S(1)}, f32[224,128]{1,0:T(8,128)S(1)}, u32[]{:S(2)}, u32[]{:S(2)}) collective-permute-start(f32[224,128]{1,0:T(8,128)S(1)} %get-tuple-element.42), channel_id=1, source_target_pairs={{0,8},{8,16},{16,24},{24,32},{32,40},{40,48},{48,56},{56,64},{64,7... | collective-permute-start | bytes 344072 | tf_op jit(solution)/shard_map/ppermute | solution.py:884
  7.1 0.0 collective-permute-start.1
  7.1 3.7 %early.1 = (f32[38,2,48,128]{3,2,1,0:T(8,128)S(1)}, f32[38,2,48,128]{3,2,1,0:T(8,128)S(1)}, f32[38,2,48,128]{3,2,1,0:T(8,128)S(1)}, f32[38,2,48,128]{3,2,1,0:T(8...) custom-call(f32[2,38,2,64,128]{4,3,2,1,0:T(8,128)S(1)} %get-tuple-el, ...), custom_call_target="tpu_custom_call" | custom-call | flops 12000000 | bytes 14000000 | tf_op jit(solution)/shard_map/early/pallas_call | solution.py:858
  10.9 0.0 collective-permute-done.from_west
  10.9 1.4 %collective-permute-done.1.from_east = f32[224,128]{1,0:T(8,128)S(1)} collective-permute-done((f32[224,128]{1,0:T(8,128)S(1)}, f32[224,128]{1,0:T(8,128)S(1)}, u32[]{:S(2)}, u32[]{:S(2)}) %collective-permute-start.1) | collective-permute-done | bytes 114720 | tf_op jit(solution)/shard_map/ppermute | solution.py:885
  12.3 1.2 %corner.1 = (f32[3,48,128]{2,1,0:T(8,128)S(1)}, f32[944,128]{1,0:T(8,128)S(1)}, f32[944,128]{1,0:T(8,128)S(1)}, f32[38,2,48,128]{3,2,1,0:T(8,128)S(1)}, f32[38,2...) custom-call(f32[224,128]{1,0:T(8,128)S(1)} %collective-permute-done., ...), custom_call_target="tpu_custom_call", output_to_operand_aliasing={{0}: (8, {}), {1}: (9, {}), {2}: (10, {}), {3}: (11, {}), {... | custom-call | tf_op jit(solution)/shard_map/corner/pallas_call | solution.py:858
  13.5 4.4 %collective-permute-start.2 = (f32[944,128]{1,0:T(8,128)S(1)}, f32[944,128]{1,0:T(8,128)S(1)}, u32[]{:S(2)}, u32[]{:S(2)}) collective-permute-start(f32[944,128]{1,0:T(8,128)S(1)} %get-tuple-element.58), channel_id=1, source_target_pairs={{0,8},{1,2},{2,1},{3,4},{4,3},{5,6},{6,5},{7,127},{8,0},{9,10},{10... | collective-permute-start | bytes 1449992 | tf_op jit(solution)/shard_map/ppermute | solution.py:913
  17.9 0.0 collective-permute-start.3
  17.9 10.6 %inner.1 = (f32[2,38,2,64,128]{4,3,2,1,0:T(8,128)S(1)}, f32[2,38,2,64,128]{4,3,2,1,0:T(8,128)S(1)}, f32[38,2,48,128]{3,2,1,0:T(8,128)S(1)}, f32[38,2,48,128]{3,2...) custom-call(f32[2,38,2,64,128]{4,3,2,1,0:T(8,128)S(1)} %get-tuple-el, ...), custom_call_target="tpu_custom_call", output_to_operand_aliasing={{0}: (0, {}), {1}: (1, {}), {2}: (2, {}), {3}: (3, {}), {4}... | custom-call | flops 60000000 | bytes 20000000 | tf_op jit(solution)/shard_map/inner/pallas_call | solution.py:858
  28.4 0.9 %collective-permute-done.2.got_second = f32[944,128]{1,0:T(8,128)S(1)} collective-permute-done((f32[944,128]{1,0:T(8,128)S(1)}, f32[944,128]{1,0:T(8,128)S(1)}, u32[]{:S(2)}, u32[]{:S(2)}) %collective-permute-start.2) | collective-permute-done | bytes 483360 | tf_op jit(solution)/shard_map/ppermute | solution.py:913
  29.3 1.5 %collective-permute-done.3.got_first = f32[944,128]{1,0:T(8,128)S(1)} collective-permute-done((f32[944,128]{1,0:T(8,128)S(1)}, f32[944,128]{1,0:T(8,128)S(1)}, u32[]{:S(2)}, u32[]{:S(2)}) %collective-permute-start.3) | collective-permute-done | bytes 483360 | tf_op jit(solution)/shard_map/ppermute | solution.py:914
  30.8 3.1 %rim.1 = (f32[2,38,2,64,128]{4,3,2,1,0:T(8,128)S(1)}, f32[2,38,2,64,128]{4,3,2,1,0:T(8,128)S(1)}, f32[38,2,48,128]{3,2,1,0:T(8,128)S(1)}, f32[38,2,48,128]{3,2,1...) custom-call(f32[944,128]{1,0:T(8,128)S(1)} %collective-permute-done., ...), custom_call_target="tpu_custom_call", output_to_operand_aliasing={{0}: (2, {}), {1}: (3, {}), {2}: (4, {}), {3}: (5, {}), {4}... | custom-call | tf_op jit(solution)/shard_map/rim/pallas_call | solution.py:858
Async XLA Ops:
  4.9 5.9 %collective-permute-start = (f32[224,128]{1,0:T(8,128)S(1)}, f32[224,128]{1,0:T(8,128)S(1)}, u32[]{:S(2)}, u32[]{:S(2)}) collective-permute-start(f32[224,128]{1,0:T(8,128)S(1)} %get-tuple-element.42), channel_id=1, source_target_pairs={{0,8},{8,16},{16,24},{24,32},{32,40},{40,48},{48,56},{56,64},{64,7... | collective-permute-start | bytes 344072 | tf_op jit(solution)/shard_map/ppermute | solution.py:884
  7.1 5.1 %collective-permute-start.1 = (f32[224,128]{1,0:T(8,128)S(1)}, f32[224,128]{1,0:T(8,128)S(1)}, u32[]{:S(2)}, u32[]{:S(2)}) collective-permute-start(f32[224,128]{1,0:T(8,128)S(1)} %get-tuple-element.43), channel_id=1, source_target_pairs={{8,0},{16,8},{24,16},{32,24},{40,32},{48,40},{56,48},{64,56},{72,6... | collective-permute-start | bytes 344072 | tf_op jit(solution)/shard_map/ppermute | solution.py:885
  13.5 15.8 %collective-permute-start.2 = (f32[944,128]{1,0:T(8,128)S(1)}, f32[944,128]{1,0:T(8,128)S(1)}, u32[]{:S(2)}, u32[]{:S(2)}) collective-permute-start(f32[944,128]{1,0:T(8,128)S(1)} %get-tuple-element.58), channel_id=1, source_target_pairs={{0,8},{1,2},{2,1},{3,4},{4,3},{5,6},{6,5},{7,127},{8,0},{9,10},{10... | collective-permute-start | bytes 1449992 | tf_op jit(solution)/shard_map/ppermute | solution.py:913
  17.9 13.0 %collective-permute-start.3 = (f32[944,128]{1,0:T(8,128)S(1)}, f32[944,128]{1,0:T(8,128)S(1)}, u32[]{:S(2)}, u32[]{:S(2)}) collective-permute-start(f32[944,128]{1,0:T(8,128)S(1)} %get-tuple-element.59), channel_id=1, source_target_pairs={{0,1},{1,0},{2,3},{3,2},{4,5},{5,4},{6,7},{7,6},{8,9},{9,8},{10,11... | collective-permute-start | bytes 1449992 | tf_op jit(solution)/shard_map/ppermute | solution.py:914
